TPU v7x, 512 devices: a whole 4x8x8 slice. The times are simulated.
512 devices in a mesh: tm: 32 (over y, z_hi, core), space: 16 (over x, z_lo).
Axes of the slice: x: 4, y: 8, z: 8 (z_hi: 2, z_lo: 4; z = z_hi * 4 + z_lo), core: 2. Of those that a mesh axis runs over, the one named last changes fastest.
Arguments:
- queries: bfloat16 [64, 1024, 2048], P('tm', 'space'), may hold values from -6 to 6
- keys: bfloat16 [64, 1024, 2048], P('tm', 'space'), may hold values from -6 to 6
- values: bfloat16 [64, 1024, 2048], P('tm', 'space'), may hold values from -6 to 6
- d_queries: bfloat16 [64, 1024, 2048], P('tm', 'space'), may hold values from -6 to 6
- d_keys: bfloat16 [64, 1024, 2048], P('tm', 'space'), may hold values from -6 to 6
- d_values: bfloat16 [64, 1024, 2048], P('tm', 'space'), may hold values from -6 to 6
Outputs:
- combined: bfloat16 [64, 1024, 2048], P('tm', 'space')
- d_combined: bfloat16 [64, 1024, 2048], P('tm', 'space')
All inputs are finite; a program needn't handle non-finite values.
Results may differ from a plain program's by a relative error of at most 0.0058.
Values may be sent and summed in bfloat16 or wider, within the bound.
No kernel may reach another device: no remote copies, remote signals or barrier semaphores. Data moves between devices by JAX's collectives and lax.ppermute only.
A program may use at most 64 MiB of HBM per device.

v0:
```python
import jax
import jax.numpy as jnp
from jax import lax
from jax.sharding import PartitionSpec as P

HEAD_DIM = 64


def attend(query_rows, key_rows, value_rows, d_query, d_key, d_value):
    score_scale = HEAD_DIM ** (-0.5)
    scores = jnp.dot(query_rows, key_rows.T, preferred_element_type=jnp.float32) * score_scale
    left_pair = jnp.concatenate([d_query, query_rows], axis=-1)
    right_pair = jnp.concatenate([key_rows, d_key], axis=-1)
    tangent = jnp.dot(left_pair, right_pair.T, preferred_element_type=jnp.float32) * score_scale
    highest = jnp.max(scores, axis=-1, keepdims=True)
    weights = jnp.exp(scores - highest)
    probabilities = weights / jnp.sum(weights, axis=-1, keepdims=True)
    d_probabilities = probabilities * (
        tangent - jnp.sum(probabilities * tangent, axis=-1, keepdims=True)
    )
    probs_low = probabilities.astype(jnp.bfloat16)
    d_low = d_probabilities.astype(jnp.bfloat16)
    output = jnp.dot(probs_low, value_rows, preferred_element_type=jnp.float32)
    stacked_low = jnp.concatenate([d_low, probs_low], axis=-1)
    stacked_values = jnp.concatenate([value_rows, d_value], axis=0)
    d_output = jnp.dot(stacked_low, stacked_values, preferred_element_type=jnp.float32)
    return (output.astype(jnp.bfloat16), d_output.astype(jnp.bfloat16))


def attend_blocked(query_rows, key_rows, value_rows, d_query, d_key, d_value):
    length = query_rows.shape[0]
    block_rows = min(512, length)
    block_count = length // block_rows
    query_blocks = query_rows.reshape(block_count, block_rows, HEAD_DIM)
    d_query_blocks = d_query.reshape(block_count, block_rows, HEAD_DIM)

    def one_block(members):
        return attend(members[0], key_rows, value_rows, members[1], d_key, d_value)

    output, d_output = lax.map(one_block, (query_blocks, d_query_blocks))
    return (output.reshape(length, HEAD_DIM), d_output.reshape(length, HEAD_DIM))


def spatial_fn(arrays):
    frame_count, length, _, features = arrays[0].shape
    local_heads = features // HEAD_DIM

    def spatial_to_heads(member):
        shaped = member.reshape(frame_count, length, local_heads, HEAD_DIM).transpose(0, 2, 1, 3)
        return shaped.reshape(frame_count * local_heads, length, HEAD_DIM)

    def restore(member):
        shaped = member.reshape(frame_count, local_heads, length, HEAD_DIM).transpose(0, 2, 1, 3)
        return shaped.reshape(frame_count, length, 1, features)

    output, d_output = lax.map(
        lambda members: attend_blocked(*members),
        tuple((spatial_to_heads(member) for member in arrays)),
    )
    return (restore(output), restore(d_output))


def temporal_fn(arrays):
    frames, _, token_count, features = arrays[0].shape
    local_heads = features // HEAD_DIM

    def temporal_to_heads(member):
        shaped = member.reshape(frames, token_count, local_heads, HEAD_DIM).transpose(1, 2, 0, 3)
        return shaped.reshape(token_count * local_heads, frames, HEAD_DIM)

    def restore(member):
        shaped = member.reshape(token_count, local_heads, frames, HEAD_DIM).transpose(2, 0, 1, 3)
        return shaped.reshape(frames, 1, token_count, features)

    output, d_output = jax.vmap(attend)(*tuple((temporal_to_heads(member) for member in arrays)))
    return (restore(output), restore(d_output))


def add_round(first, second):
    return (first.astype(jnp.float32) + second.astype(jnp.float32)).astype(jnp.bfloat16)


def body(queries, keys, values, d_queries, d_keys, d_values):
    frames_dev, tok_dev, width = queries.shape
    space_count = lax.axis_size("space")
    time_count = lax.axis_size("tm")
    features = width // space_count
    arrays = (queries, keys, values, d_queries, d_keys, d_values)
    panels = tuple(
        (member.reshape(frames_dev, tok_dev, space_count, features) for member in arrays)
    )
    spatial = spatial_fn(
        (
            lax.all_to_all(panels[0], "space", split_axis=2, concat_axis=1, tiled=True),
            lax.all_to_all(panels[1], "space", split_axis=2, concat_axis=1, tiled=True),
            lax.all_to_all(panels[2], "space", split_axis=2, concat_axis=1, tiled=True),
            lax.all_to_all(panels[3], "space", split_axis=2, concat_axis=1, tiled=True),
            lax.all_to_all(panels[4], "space", split_axis=2, concat_axis=1, tiled=True),
            lax.all_to_all(panels[5], "space", split_axis=2, concat_axis=1, tiled=True),
        )
    )
    spatial_out, d_spatial_out = (
        lax.all_to_all(spatial[0], "space", split_axis=1, concat_axis=2, tiled=True),
        lax.all_to_all(spatial[1], "space", split_axis=1, concat_axis=2, tiled=True),
    )
    across = tuple(
        (member.reshape(frames_dev, time_count, tok_dev // time_count, width) for member in arrays)
    )
    temporal = temporal_fn(
        (
            lax.all_to_all(across[0], "tm", split_axis=1, concat_axis=0, tiled=True),
            lax.all_to_all(across[1], "tm", split_axis=1, concat_axis=0, tiled=True),
            lax.all_to_all(across[2], "tm", split_axis=1, concat_axis=0, tiled=True),
            lax.all_to_all(across[3], "tm", split_axis=1, concat_axis=0, tiled=True),
            lax.all_to_all(across[4], "tm", split_axis=1, concat_axis=0, tiled=True),
            lax.all_to_all(across[5], "tm", split_axis=1, concat_axis=0, tiled=True),
        )
    )
    temporal_out, d_temporal_out = (
        lax.all_to_all(temporal[0], "tm", split_axis=0, concat_axis=1, tiled=True),
        lax.all_to_all(temporal[1], "tm", split_axis=0, concat_axis=1, tiled=True),
    )
    combined = add_round(
        spatial_out.reshape(frames_dev, tok_dev, width),
        temporal_out.reshape(frames_dev, tok_dev, width),
    )
    d_combined = add_round(
        d_spatial_out.reshape(frames_dev, tok_dev, width),
        d_temporal_out.reshape(frames_dev, tok_dev, width),
    )
    return (combined, d_combined)


def solution(mesh):
    return jax.shard_map(
        body,
        mesh=mesh,
        in_specs=(
            P("tm", "space", None),
            P("tm", "space", None),
            P("tm", "space", None),
            P("tm", "space", None),
            P("tm", "space", None),
            P("tm", "space", None),
        ),
        out_specs=(P("tm", "space", None), P("tm", "space", None)),
        check_vma=False,
    )
```

profile of v0, /device:TPU:1, one launch (start us, length us, event | category | flops | bytes accessed | tf_op | source)
XLA Modules:
  0.0 465.4 jit_solution(5828384979273890703)
XLA Ops:
  2.7 10.4 %all-to-all-start = ((bf16[2,64,16,128]{3,1,0,2:T(8,128)(2,1)}), bf16[2,64,16,128]{3,1,0,2:T(8,128)(2,1)S(1)}, u32[]{:S(2)}, u32[]{:S(2)}) async-start(bf16[2,64,16,128]{3,1,0,2:T(8,128)(2,1)} %copy_bitcast_fusion.7), calls=%async_computation | async-start | bytes 1048576 | tf_op jit(solution)/shard_map/all_to_all | solution.py:94
  14.1 14.8 %all-to-all-done = bf16[2,64,16,128]{3,1,0,2:T(8,128)(2,1)S(1)} async-done(((bf16[2,64,16,128]{3,1,0,2:T(8,128)(2,1)}), bf16[2,64,16,128]{3,1,0,2:T(8,128)(2,1)S(1)}, u32[]{:S(2)}, u32[]{:S(2)}) %all-to-all-start) | async-done | bytes 524320 | tf_op jit(solution)/shard_map/all_to_all | solution.py:94
  33.4 14.7 %all-to-all-done.1 = bf16[2,64,16,128]{3,1,0,2:T(8,128)(2,1)S(1)} async-done(((bf16[2,64,16,128]{3,1,0,2:T(8,128)(2,1)}), bf16[2,64,16,128]{3,1,0,2:T(8,128)(2,1)S(1)}, u32[]{:S(2)}, u32[]{:S(2)}) %all-to-all-start.1) | async-done | bytes 524320 | tf_op jit(solution)/shard_map/all_to_all | solution.py:97
  52.6 14.7 %all-to-all-done.2 = bf16[2,64,16,128]{3,1,0,2:T(8,128)(2,1)S(1)} async-done(((bf16[2,64,16,128]{3,1,0,2:T(8,128)(2,1)}), bf16[2,64,16,128]{3,1,0,2:T(8,128)(2,1)S(1)}, u32[]{:S(2)}, u32[]{:S(2)}) %all-to-all-start.2) | async-done | bytes 524320 | tf_op jit(solution)/shard_map/all_to_all | solution.py:95
  71.8 14.7 %all-to-all-done.3 = bf16[2,64,16,128]{3,1,0,2:T(8,128)(2,1)S(1)} async-done(((bf16[2,64,16,128]{3,1,0,2:T(8,128)(2,1)}), bf16[2,64,16,128]{3,1,0,2:T(8,128)(2,1)S(1)}, u32[]{:S(2)}, u32[]{:S(2)}) %all-to-all-start.3) | async-done | bytes 524320 | tf_op jit(solution)/shard_map/all_to_all | solution.py:96
  91.1 14.7 %all-to-all-done.4 = bf16[2,64,16,128]{3,1,0,2:T(8,128)(2,1)S(1)} async-done(((bf16[2,64,16,128]{3,1,0,2:T(8,128)(2,1)}), bf16[2,64,16,128]{3,1,0,2:T(8,128)(2,1)S(1)}, u32[]{:S(2)}, u32[]{:S(2)}) %all-to-all-start.4) | async-done | bytes 524320 | tf_op jit(solution)/shard_map/all_to_all | solution.py:98
  105.8 3.7 all-to-all-start.5
  114.1 11.1 %all-to-all-done.5 = bf16[2,64,16,128]{3,1,0,2:T(8,128)(2,1)S(1)} async-done(((bf16[2,64,16,128]{3,1,0,2:T(8,128)(2,1)}), bf16[2,64,16,128]{3,1,0,2:T(8,128)(2,1)S(1)}, u32[]{:S(2)}, u32[]{:S(2)}) %all-to-all-start.5) | async-done | bytes 524320 | tf_op jit(solution)/shard_map/all_to_all | solution.py:99
  125.2 14.8 %all-to-all-start.14 = ((bf16[2,32,2,2048]{3,2,0,1:T(2,128)(2,1)}), bf16[2,32,2,2048]{3,2,0,1:T(2,128)(2,1)S(1)}, u32[]{:S(2)}, u32[]{:S(2)}) async-start(bf16[2,32,2,2048]{3,2,0,1:T(2,128)(2,1)} %copy.172), calls=%async_computation.14 | async-start | bytes 1048576 | tf_op jit(solution)/shard_map/all_to_all | solution.py:116
  141.7 16.6 %all-to-all-done.14 = bf16[2,32,2,2048]{3,2,0,1:T(2,128)(2,1)S(1)} async-done(((bf16[2,32,2,2048]{3,2,0,1:T(2,128)(2,1)}), bf16[2,32,2,2048]{3,2,0,1:T(2,128)(2,1)S(1)}, u32[]{:S(2)}, u32[]{:S(2)}) %all-to-all-start.14) | async-done | bytes 524320 | tf_op jit(solution)/shard_map/all_to_all | solution.py:116
  158.3 6.7 %all-to-all-start.9 = ((bf16[2,32,2,2048]{3,2,0,1:T(2,128)(2,1)}), bf16[2,32,2,2048]{3,2,0,1:T(2,128)(2,1)S(1)}, u32[]{:S(2)}, u32[]{:S(2)}) async-start(bf16[2,32,2,2048]{3,2,0,1:T(2,128)(2,1)} %copy.158), calls=%async_computation.9 | async-start | bytes 1048576 | tf_op jit(solution)/shard_map/all_to_all | solution.py:113
  166.8 16.6 %all-to-all-done.9 = bf16[2,32,2,2048]{3,2,0,1:T(2,128)(2,1)S(1)} async-done(((bf16[2,32,2,2048]{3,2,0,1:T(2,128)(2,1)}), bf16[2,32,2,2048]{3,2,0,1:T(2,128)(2,1)S(1)}, u32[]{:S(2)}, u32[]{:S(2)}) %all-to-all-start.9) | async-done | bytes 524320 | tf_op jit(solution)/shard_map/all_to_all | solution.py:113
  183.4 6.7 %all-to-all-start.7 = ((bf16[2,32,2,2048]{3,2,0,1:T(2,128)(2,1)}), bf16[2,32,2,2048]{3,2,0,1:T(2,128)(2,1)S(1)}, u32[]{:S(2)}, u32[]{:S(2)}) async-start(bf16[2,32,2,2048]{3,2,0,1:T(2,128)(2,1)} %copy.154), calls=%async_computation.7 | async-start | bytes 1048576 | tf_op jit(solution)/shard_map/all_to_all | solution.py:111
  191.9 16.6 %all-to-all-done.7 = bf16[2,32,2,2048]{3,2,0,1:T(2,128)(2,1)S(1)} async-done(((bf16[2,32,2,2048]{3,2,0,1:T(2,128)(2,1)}), bf16[2,32,2,2048]{3,2,0,1:T(2,128)(2,1)S(1)}, u32[]{:S(2)}, u32[]{:S(2)}) %all-to-all-start.7) | async-done | bytes 524320 | tf_op jit(solution)/shard_map/all_to_all | solution.py:111
  208.5 6.7 %all-to-all-start.8 = ((bf16[2,32,2,2048]{3,2,0,1:T(2,128)(2,1)}), bf16[2,32,2,2048]{3,2,0,1:T(2,128)(2,1)S(1)}, u32[]{:S(2)}, u32[]{:S(2)}) async-start(bf16[2,32,2,2048]{3,2,0,1:T(2,128)(2,1)} %copy.156), calls=%async_computation.8 | async-start | bytes 1048576 | tf_op jit(solution)/shard_map/all_to_all | solution.py:112
  218.8 14.8 %all-to-all-done.8 = bf16[2,32,2,2048]{3,2,0,1:T(2,128)(2,1)S(1)} async-done(((bf16[2,32,2,2048]{3,2,0,1:T(2,128)(2,1)}), bf16[2,32,2,2048]{3,2,0,1:T(2,128)(2,1)S(1)}, u32[]{:S(2)}, u32[]{:S(2)}) %all-to-all-start.8) | async-done | bytes 524320 | tf_op jit(solution)/shard_map/all_to_all | solution.py:112
  233.6 7.5 %all-to-all-start.12 = ((bf16[2,32,2,2048]{3,2,0,1:T(2,128)(2,1)}), bf16[2,32,2,2048]{3,2,0,1:T(2,128)(2,1)}, u32[]{:S(2)}, u32[]{:S(2)}) async-start(bf16[2,32,2,2048]{3,2,0,1:T(2,128)(2,1)} %copy.168), calls=%async_computation.12 | async-start | bytes 1048576 | tf_op jit(solution)/shard_map/all_to_all | solution.py:114
  255.7 3.7 all-to-all-done.12
  259.4 8.9 %all-to-all-start.13 = ((bf16[2,32,2,2048]{3,2,0,1:T(2,128)(2,1)}), bf16[2,32,2,2048]{3,2,0,1:T(2,128)(2,1)}, u32[]{:S(2)}, u32[]{:S(2)}) async-start(bf16[2,32,2,2048]{3,2,0,1:T(2,128)(2,1)} %copy.170), calls=%async_computation.13 | async-start | bytes 1048576 | tf_op jit(solution)/shard_map/all_to_all | solution.py:115
  268.3 52.6 %while.27 = (s32[]{:T(128)}, bf16[4,1024,64]{1,2,0:T(8,128)(2,1)}, bf16[4,1024,64]{1,2,0:T(8,128)(2,1)}, bf16[4,1024,64]{1,2,0:T(8,128)(2,1)S(1)}, bf16[4,1024,6...) while((s32[]{:T(128)}, bf16[4,1024,64]{1,2,0:T(8,128)(2,1)}, ...), condition=%wide.region_6.7_spmd, body=%wide.region_0.6_spmd.sunk | while | flops 418183680 | bytes 33769944 | solution.py:56
  271.8 8.3 %while.28 = (s32[]{:T(128)}, bf16[2,512,64]{1,2,0:T(8,128)(2,1)S(1)}, bf16[2,512,64]{1,2,0:T(8,128)(2,1)S(1)}, bf16[2,512,64]{2,1,0:T(8,128)(2,1)S(1)}, bf16[102...) while((s32[]{:T(128)}, ...), condition=%wide.region_5.5_spmd, body=%wide.region_1.4_spmd.sunk | while | flops 417135104 | bytes 19613816 | solution.py:40
  284.9 8.3 %while.28 = (s32[]{:T(128)}, bf16[2,512,64]{1,2,0:T(8,128)(2,1)S(1)}, bf16[2,512,64]{1,2,0:T(8,128)(2,1)S(1)}, bf16[2,512,64]{2,1,0:T(8,128)(2,1)S(1)}, bf16[102...) while((s32[]{:T(128)}, ...), condition=%wide.region_5.5_spmd, body=%wide.region_1.4_spmd.sunk | while | flops 417135104 | bytes 19613816 | solution.py:40
  298.1 8.3 %while.28 = (s32[]{:T(128)}, bf16[2,512,64]{1,2,0:T(8,128)(2,1)S(1)}, bf16[2,512,64]{1,2,0:T(8,128)(2,1)S(1)}, bf16[2,512,64]{2,1,0:T(8,128)(2,1)S(1)}, bf16[102...) while((s32[]{:T(128)}, ...), condition=%wide.region_5.5_spmd, body=%wide.region_1.4_spmd.sunk | while | flops 417135104 | bytes 19613816 | solution.py:40
  311.2 8.3 %while.28 = (s32[]{:T(128)}, bf16[2,512,64]{1,2,0:T(8,128)(2,1)S(1)}, bf16[2,512,64]{1,2,0:T(8,128)(2,1)S(1)}, bf16[2,512,64]{2,1,0:T(8,128)(2,1)S(1)}, bf16[102...) while((s32[]{:T(128)}, ...), condition=%wide.region_5.5_spmd, body=%wide.region_1.4_spmd.sunk | while | flops 417135104 | bytes 19613816 | solution.py:40
  323.1 4.2 all-to-all-start.11
  333.4 10.1 %all-to-all-done.11 = bf16[2,1024,1,128]{3,0,2,1:T(2,128)(2,1)} async-done(((bf16[2,1024,1,128]{3,0,2,1:T(2,128)(2,1)}), bf16[2,1024,1,128]{3,0,2,1:T(2,128)(2,1)}, u32[]{:S(2)}, u32[]{:S(2)}) %all-to-all-start.11) | async-done | bytes 524320 | tf_op jit(solution)/shard_map/all_to_all | solution.py:104
  343.5 4.4 all-to-all-start.6
  374.3 22.5 %multiply_convert_fusion.1 = bf16[64,64,64]{2,1,0:T(8,128)(2,1)S(1)} fusion(f32[64,64,64]{2,1,0:T(8,128)S(1)} %fusion.38, f32[64,64,64]{2,1,0:T(8,128)S(1)} %copy-done, f32[64,64]{1,0:T(8,128)S(1)} %get-tuple-element.244), kind=kOutput, calls=%fused_computation.41 | output fusion | flops 2101311 | bytes 2637824 | tf_op jit(solution)/shard_map/vmap()/sub | solution.py:19
  402.7 13.1 %all-to-all-start.15 = ((bf16[64,1,2,2048]{3,2,1,0:T(2,128)(2,1)}), bf16[64,1,2,2048]{3,2,1,0:T(2,128)(2,1)S(1)}, u32[]{:S(2)}, u32[]{:S(2)}) async-start(bf16[64,1,2,2048]{3,2,1,0:T(2,128)(2,1)} %copy.176), calls=%async_computation.15 | async-start | bytes 1048576 | tf_op jit(solution)/shard_map/all_to_all | solution.py:121
  420.2 14.6 %all-to-all-done.15 = bf16[64,1,2,2048]{3,2,1,0:T(2,128)(2,1)S(1)} async-done(((bf16[64,1,2,2048]{3,2,1,0:T(2,128)(2,1)}), bf16[64,1,2,2048]{3,2,1,0:T(2,128)(2,1)S(1)}, u32[]{:S(2)}, u32[]{:S(2)}) %all-to-all-start.15) | async-done | bytes 524320 | tf_op jit(solution)/shard_map/all_to_all | solution.py:121
  434.8 6.6 %all-to-all-start.10 = ((bf16[64,1,2,2048]{3,2,1,0:T(2,128)(2,1)}), bf16[64,1,2,2048]{3,2,1,0:T(2,128)(2,1)}, u32[]{:S(2)}, u32[]{:S(2)}) async-start(bf16[64,1,2,2048]{3,2,1,0:T(2,128)(2,1)} %copy.161), calls=%async_computation.10 | async-start | bytes 1048576 | tf_op jit(solution)/shard_map/all_to_all | solution.py:120
  446.8 13.6 %all-to-all-done.10 = bf16[64,1,2,2048]{3,2,1,0:T(2,128)(2,1)} async-done(((bf16[64,1,2,2048]{3,2,1,0:T(2,128)(2,1)}), bf16[64,1,2,2048]{3,2,1,0:T(2,128)(2,1)}, u32[]{:S(2)}, u32[]{:S(2)}) %all-to-all-start.10) | async-done | bytes 524320 | tf_op jit(solution)/shard_map/all_to_all | solution.py:120
  (304 shorter events, 155.0 us)
Async XLA Ops:
  0.6 31.8 %copy-start.24 = (bf16[2,64,2048]{2,1,0:T(8,128)(2,1)S(1)}, bf16[2,64,2048]{2,1,0:T(8,128)(2,1)}, u32[]{:S(2)}) copy-start(bf16[2,64,2048]{2,1,0:T(8,128)(2,1)} %param.11) | copy-start | bytes 1572868
  2.7 26.1 %all-to-all-start = ((bf16[2,64,16,128]{3,1,0,2:T(8,128)(2,1)}), bf16[2,64,16,128]{3,1,0,2:T(8,128)(2,1)S(1)}, u32[]{:S(2)}, u32[]{:S(2)}) async-start(bf16[2,64,16,128]{3,1,0,2:T(8,128)(2,1)} %copy_bitcast_fusion.7), calls=%async_computation | async-start | bytes 1048576 | tf_op jit(solution)/shard_map/all_to_all | solution.py:94
  13.1 38.5 %copy-start.21 = (bf16[2,64,2048]{2,1,0:T(8,128)(2,1)S(1)}, bf16[2,64,2048]{2,1,0:T(8,128)(2,1)}, u32[]{:S(2)}) copy-start(bf16[2,64,2048]{2,1,0:T(8,128)(2,1)} %param.12) | copy-start | bytes 1572868
  28.8 19.2 %all-to-all-start.1 = ((bf16[2,64,16,128]{3,1,0,2:T(8,128)(2,1)}), bf16[2,64,16,128]{3,1,0,2:T(8,128)(2,1)S(1)}, u32[]{:S(2)}, u32[]{:S(2)}) async-start(bf16[2,64,16,128]{3,1,0,2:T(8,128)(2,1)} %copy_bitcast_fusion.6), calls=%async_computation.1 | async-start | bytes 1048576 | tf_op jit(solution)/shard_map/all_to_all | solution.py:97
  32.4 38.5 %copy-start.28 = (bf16[2,64,2048]{2,1,0:T(8,128)(2,1)S(1)}, bf16[2,64,2048]{2,1,0:T(8,128)(2,1)}, u32[]{:S(2)}) copy-start(bf16[2,64,2048]{2,1,0:T(8,128)(2,1)} %param.14) | copy-start | bytes 1572868
  48.1 19.2 %all-to-all-start.2 = ((bf16[2,64,16,128]{3,1,0,2:T(8,128)(2,1)}), bf16[2,64,16,128]{3,1,0,2:T(8,128)(2,1)S(1)}, u32[]{:S(2)}, u32[]{:S(2)}) async-start(bf16[2,64,16,128]{3,1,0,2:T(8,128)(2,1)} %copy_bitcast_fusion.5), calls=%async_computation.2 | async-start | bytes 1048576 | tf_op jit(solution)/shard_map/all_to_all | solution.py:95
  51.7 38.5 %copy-start.20 = (bf16[2,64,2048]{2,1,0:T(8,128)(2,1)S(1)}, bf16[2,64,2048]{2,1,0:T(8,128)(2,1)}, u32[]{:S(2)}) copy-start(bf16[2,64,2048]{2,1,0:T(8,128)(2,1)} %param.15) | copy-start | bytes 1572868
  67.3 23.8 %copy-start.13 = (bf16[2,64,16,128]{3,1,0,2:T(8,128)(2,1)}, bf16[2,64,16,128]{3,1,0,2:T(8,128)(2,1)S(1)}, u32[]{:S(2)}) copy-start(bf16[2,64,16,128]{3,1,0,2:T(8,128)(2,1)S(1)} %all-to-all-done.2) | copy-start | bytes 1572868
  67.3 19.2 %all-to-all-start.3 = ((bf16[2,64,16,128]{3,1,0,2:T(8,128)(2,1)}), bf16[2,64,16,128]{3,1,0,2:T(8,128)(2,1)S(1)}, u32[]{:S(2)}, u32[]{:S(2)}) async-start(bf16[2,64,16,128]{3,1,0,2:T(8,128)(2,1)} %copy_bitcast_fusion.4), calls=%async_computation.3 | async-start | bytes 1048576 | tf_op jit(solution)/shard_map/all_to_all | solution.py:96
  86.5 25.1 %copy-start.15 = (bf16[2,64,16,128]{3,1,0,2:T(8,128)(2,1)}, bf16[2,64,16,128]{3,1,0,2:T(8,128)(2,1)S(1)}, u32[]{:S(2)}) copy-start(bf16[2,64,16,128]{3,1,0,2:T(8,128)(2,1)S(1)} %all-to-all-done.3) | copy-start | bytes 1572868
  86.5 19.2 %all-to-all-start.4 = ((bf16[2,64,16,128]{3,1,0,2:T(8,128)(2,1)}), bf16[2,64,16,128]{3,1,0,2:T(8,128)(2,1)S(1)}, u32[]{:S(2)}, u32[]{:S(2)}) async-start(bf16[2,64,16,128]{3,1,0,2:T(8,128)(2,1)} %copy_bitcast_fusion.3), calls=%async_computation.4 | async-start | bytes 1048576 | tf_op jit(solution)/shard_map/all_to_all | solution.py:98
  105.8 34.2 %copy-start.22 = (bf16[2,64,2048]{2,1,0:T(8,128)(2,1)S(1)}, bf16[2,64,2048]{2,1,0:T(8,128)(2,1)}, u32[]{:S(2)}) copy-start(bf16[2,64,2048]{2,1,0:T(8,128)(2,1)} %param.12) | copy-start | bytes 1572868
  105.8 19.4 %all-to-all-start.5 = ((bf16[2,64,16,128]{3,1,0,2:T(8,128)(2,1)}), bf16[2,64,16,128]{3,1,0,2:T(8,128)(2,1)S(1)}, u32[]{:S(2)}, u32[]{:S(2)}) async-start(bf16[2,64,16,128]{3,1,0,2:T(8,128)(2,1)} %copy_bitcast_fusion.2), calls=%async_computation.5 | async-start | bytes 1048576 | tf_op jit(solution)/shard_map/all_to_all | solution.py:99
  125.2 33.1 %copy-start.18 = (bf16[2,64,16,128]{3,1,0,2:T(8,128)(2,1)}, bf16[2,64,16,128]{3,1,0,2:T(8,128)(2,1)S(1)}, u32[]{:S(2)}) copy-start(bf16[2,64,16,128]{3,1,0,2:T(8,128)(2,1)S(1)} %all-to-all-done.5) | copy-start | bytes 1572868
  125.2 33.1 %all-to-all-start.14 = ((bf16[2,32,2,2048]{3,2,0,1:T(2,128)(2,1)}), bf16[2,32,2,2048]{3,2,0,1:T(2,128)(2,1)S(1)}, u32[]{:S(2)}, u32[]{:S(2)}) async-start(bf16[2,32,2,2048]{3,2,0,1:T(2,128)(2,1)} %copy.172), calls=%async_computation.14 | async-start | bytes 1048576 | tf_op jit(solution)/shard_map/all_to_all | solution.py:116
  140.3 24.8 %copy-start.23 = (bf16[2,64,2048]{2,1,0:T(8,128)(2,1)S(1)}, bf16[2,64,2048]{2,1,0:T(8,128)(2,1)}, u32[]{:S(2)}) copy-start(bf16[2,64,2048]{2,1,0:T(8,128)(2,1)} %param.10) | copy-start | bytes 1572868
  158.3 25.1 %copy-start.7 = (bf16[2,32,2,2048]{3,2,0,1:T(2,128)(2,1)}, bf16[2,32,2,2048]{3,2,0,1:T(2,128)(2,1)S(1)}, u32[]{:S(2)}) copy-start(bf16[2,32,2,2048]{3,2,0,1:T(2,128)(2,1)S(1)} %all-to-all-done.14) | copy-start | bytes 1572868
  158.3 25.1 %all-to-all-start.9 = ((bf16[2,32,2,2048]{3,2,0,1:T(2,128)(2,1)}), bf16[2,32,2,2048]{3,2,0,1:T(2,128)(2,1)S(1)}, u32[]{:S(2)}, u32[]{:S(2)}) async-start(bf16[2,32,2,2048]{3,2,0,1:T(2,128)(2,1)} %copy.158), calls=%async_computation.9 | async-start | bytes 1048576 | tf_op jit(solution)/shard_map/all_to_all | solution.py:113
  165.4 24.8 %copy-start.25 = (bf16[2,64,2048]{2,1,0:T(8,128)(2,1)S(1)}, bf16[2,64,2048]{2,1,0:T(8,128)(2,1)}, u32[]{:S(2)}) copy-start(bf16[2,64,2048]{2,1,0:T(8,128)(2,1)} %param.11) | copy-start | bytes 1572868
  183.4 25.1 %copy-start.8 = (bf16[2,32,2,2048]{3,2,0,1:T(2,128)(2,1)}, bf16[2,32,2,2048]{3,2,0,1:T(2,128)(2,1)S(1)}, u32[]{:S(2)}) copy-start(bf16[2,32,2,2048]{3,2,0,1:T(2,128)(2,1)S(1)} %all-to-all-done.9) | copy-start | bytes 1572868
  183.4 25.1 %all-to-all-start.7 = ((bf16[2,32,2,2048]{3,2,0,1:T(2,128)(2,1)}), bf16[2,32,2,2048]{3,2,0,1:T(2,128)(2,1)S(1)}, u32[]{:S(2)}, u32[]{:S(2)}) async-start(bf16[2,32,2,2048]{3,2,0,1:T(2,128)(2,1)} %copy.154), calls=%async_computation.7 | async-start | bytes 1048576 | tf_op jit(solution)/shard_map/all_to_all | solution.py:111
  190.5 24.8 %copy-start.27 = (bf16[2,64,2048]{2,1,0:T(8,128)(2,1)S(1)}, bf16[2,64,2048]{2,1,0:T(8,128)(2,1)}, u32[]{:S(2)}) copy-start(bf16[2,64,2048]{2,1,0:T(8,128)(2,1)} %param.13) | copy-start | bytes 1572868
  208.5 32.6 %copy-start.9 = (bf16[2,32,2,2048]{3,2,0,1:T(2,128)(2,1)}, bf16[2,32,2,2048]{3,2,0,1:T(2,128)(2,1)S(1)}, u32[]{:S(2)}) copy-start(bf16[2,32,2,2048]{3,2,0,1:T(2,128)(2,1)S(1)} %all-to-all-done.7) | copy-start | bytes 1572868
  208.5 25.1 %all-to-all-start.8 = ((bf16[2,32,2,2048]{3,2,0,1:T(2,128)(2,1)}), bf16[2,32,2,2048]{3,2,0,1:T(2,128)(2,1)S(1)}, u32[]{:S(2)}, u32[]{:S(2)}) async-start(bf16[2,32,2,2048]{3,2,0,1:T(2,128)(2,1)} %copy.156), calls=%async_computation.8 | async-start | bytes 1048576 | tf_op jit(solution)/shard_map/all_to_all | solution.py:112
  215.3 25.9 %copy-start.29 = (bf16[2,64,2048]{2,1,0:T(8,128)(2,1)S(1)}, bf16[2,64,2048]{2,1,0:T(8,128)(2,1)}, u32[]{:S(2)}) copy-start(bf16[2,64,2048]{2,1,0:T(8,128)(2,1)} %param.14) | copy-start | bytes 1572868
  233.6 25.7 %all-to-all-start.12 = ((bf16[2,32,2,2048]{3,2,0,1:T(2,128)(2,1)}), bf16[2,32,2,2048]{3,2,0,1:T(2,128)(2,1)}, u32[]{:S(2)}, u32[]{:S(2)}) async-start(bf16[2,32,2,2048]{3,2,0,1:T(2,128)(2,1)} %copy.168), calls=%async_computation.12 | async-start | bytes 1048576 | tf_op jit(solution)/shard_map/all_to_all | solution.py:114
  259.4 63.7 %all-to-all-start.13 = ((bf16[2,32,2,2048]{3,2,0,1:T(2,128)(2,1)}), bf16[2,32,2,2048]{3,2,0,1:T(2,128)(2,1)}, u32[]{:S(2)}, u32[]{:S(2)}) async-start(bf16[2,32,2,2048]{3,2,0,1:T(2,128)(2,1)} %copy.170), calls=%async_computation.13 | async-start | bytes 1048576 | tf_op jit(solution)/shard_map/all_to_all | solution.py:115
  323.1 20.5 %all-to-all-start.11 = ((bf16[2,1024,1,128]{3,0,2,1:T(2,128)(2,1)}), bf16[2,1024,1,128]{3,0,2,1:T(2,128)(2,1)}, u32[]{:S(2)}, u32[]{:S(2)}) async-start(bf16[2,1024,1,128]{3,0,2,1:T(2,128)(2,1)} %copy.165), calls=%async_computation.11 | async-start | bytes 1048576 | tf_op jit(solution)/shard_map/all_to_all | solution.py:104
  343.5 59.2 %all-to-all-start.6 = ((bf16[2,1024,1,128]{3,0,2,1:T(2,128)(2,1)}), bf16[2,1024,1,128]{3,0,2,1:T(2,128)(2,1)}, u32[]{:S(2)}, u32[]{:S(2)}) async-start(bf16[2,1024,1,128]{3,0,2,1:T(2,128)(2,1)} %copy.151), calls=%async_computation.6 | async-start | bytes 1048576 | tf_op jit(solution)/shard_map/all_to_all | solution.py:103
  374.3 22.5 %copy-start.30 = (bf16[2,32,64,64]{3,2,1,0:T(8,128)(2,1)S(1)}, bf16[2,32,64,64]{3,2,1,0:T(8,128)(2,1)}, u32[]{:S(2)}) copy-start(bf16[2,32,64,64]{3,2,1,0:T(8,128)(2,1)} %copy.173) | copy-start | bytes 1572868
  402.7 32.1 %all-to-all-start.15 = ((bf16[64,1,2,2048]{3,2,1,0:T(2,128)(2,1)}), bf16[64,1,2,2048]{3,2,1,0:T(2,128)(2,1)S(1)}, u32[]{:S(2)}, u32[]{:S(2)}) async-start(bf16[64,1,2,2048]{3,2,1,0:T(2,128)(2,1)} %copy.176), calls=%async_computation.15 | async-start | bytes 1048576 | tf_op jit(solution)/shard_map/all_to_all | solution.py:121
  434.8 25.5 %all-to-all-start.10 = ((bf16[64,1,2,2048]{3,2,1,0:T(2,128)(2,1)}), bf16[64,1,2,2048]{3,2,1,0:T(2,128)(2,1)}, u32[]{:S(2)}, u32[]{:S(2)}) async-start(bf16[64,1,2,2048]{3,2,1,0:T(2,128)(2,1)} %copy.161), calls=%async_computation.10 | async-start | bytes 1048576 | tf_op jit(solution)/shard_map/all_to_all | solution.py:120
  (28 other events, 117.3 us)
where the time goes:
time: 474 us; the launch traced here: 465 us
  waiting for transfers between devices  191 us (40%)
  starting transfers between devices  108 us (23%)
  local copies, waits for them, and re-layouts  94.3 us (20%)
  other arithmetic  40.9 us (9%)
  matrix products  28.1 us (6%)
    sub x1, other arithmetic, attend(): tangent - jnp.sum(probabilities * tangent, axis=-1, keepdims=True)  22.5 us
    all_to_all x1, waiting for transfers between devices, body(): lax.all_to_all(across[5], 'tm', split_axis=1, concat_axis=0, tiled=True)  16.6 us
    all_to_all x1, waiting for transfers between devices, body(): lax.all_to_all(across[2], 'tm', split_axis=1, concat_axis=0, tiled=True)  16.6 us
    all_to_all x1, waiting for transfers between devices, body(): lax.all_to_all(across[0], 'tm', split_axis=1, concat_axis=0, tiled=True)  16.6 us
    reshape x12, local copies, waits for them, and re-layouts, body(): member.reshape(frames_dev, time_count, tok_dev // time_count, width)  14.9 us
    all_to_all x1, waiting for transfers between devices, body(): lax.all_to_all(across[1], 'tm', split_axis=1, concat_axis=0, tiled=True)  14.8 us
    all_to_all x1, starting transfers between devices, body(): lax.all_to_all(across[5], 'tm', split_axis=1, concat_axis=0, tiled=True)  14.8 us
    all_to_all x1, waiting for transfers between devices, body(): lax.all_to_all(panels[0], 'space', split_axis=2, concat_axis=1, tiled=True)  14.8 us
  transfers between devices with their start and end apart: 16, of which 14 were waited for; matrix products, arithmetic and copies ran while one was open for 33% of the time, Pallas kernels for 0%

commit v1 on v0

v1 whole, which is shorter than its diff:
```python
import functools
import jax
import jax.numpy as jnp
from jax import lax
from jax.experimental import pallas as pl
from jax.experimental.pallas import tpu as pltpu
from jax.sharding import PartitionSpec as P

HEAD_DIM = 64
LANES = 128
F32 = jnp.float32
BF16 = jnp.bfloat16
VMEM_LIMIT = 50 * 1024 * 1024


def params():
    return pltpu.CompilerParams(vmem_limit_bytes=VMEM_LIMIT)


def dot_t(a, b):
    return lax.dot_general(a, b, (((1,), (1,)), ((), ())), preferred_element_type=F32)


def dot(a, b):
    return jnp.dot(a, b, preferred_element_type=F32)


def pack_space_kernel(*refs):
    out = refs[6]
    for a in range(6):
        out[0, a] = refs[a][...]


def pack_space(arrays):
    frames, tokens, width = arrays[0].shape
    pairs = width // LANES
    return pl.pallas_call(
        pack_space_kernel,
        grid=(pairs,),
        in_specs=[pl.BlockSpec((frames, tokens, LANES), lambda d: (0, 0, d))] * 6,
        out_specs=pl.BlockSpec((1, 6, frames, tokens, LANES), lambda d: (d, 0, 0, 0, 0)),
        out_shape=jax.ShapeDtypeStruct((pairs, 6, frames, tokens, LANES), BF16),
        compiler_params=params(),
        cost_estimate=pl.CostEstimate(flops=0, bytes_accessed=6 << 20, transcendentals=0),
        name="pack_space",
    )(*arrays)


def pack_time_kernel(*refs):
    out = refs[6]
    groups = out.shape[0]
    for a in range(6):
        for pair in range(2):
            for f in range(2):
                for g in range(groups):
                    out[g, 0, a, pair, f] = refs[a][f, g * 16:(g + 1) * 16, pair * LANES:(pair + 1) * LANES]


def pack_time(arrays):
    frames, tokens, width = arrays[0].shape
    groups, lane_groups = tokens // 16, width // 256
    return pl.pallas_call(
        pack_time_kernel,
        grid=(lane_groups,),
        in_specs=[pl.BlockSpec((frames, tokens, 256), lambda d: (0, 0, d))] * 6,
        out_specs=pl.BlockSpec((groups, 1, 6, 2, frames, 16, LANES), lambda d: (0, d, 0, 0, 0, 0, 0)),
        out_shape=jax.ShapeDtypeStruct((groups, lane_groups, 6, 2, frames, 16, LANES), BF16),
        compiler_params=params(),
        cost_estimate=pl.CostEstimate(flops=0, bytes_accessed=6 << 20, transcendentals=0),
        name="pack_time",
    )(*arrays)


def soft_parts(s, ds):
    e = jnp.exp(s - jnp.max(s, axis=-1, keepdims=True))
    p = e * (1.0 / jnp.sum(e, axis=-1, keepdims=True))
    dp = p * (ds - jnp.sum(p * ds, axis=-1, keepdims=True))
    return p.astype(BF16), dp.astype(BF16)


def spatial_kernel(q_ref, dq_ref, k_ref, v_ref, dk_ref, dv_ref, out_ref):
    rows = q_ref.shape[0] * q_ref.shape[3]
    keys = k_ref.shape[0] * k_ref.shape[3]
    q = q_ref[...].reshape(rows, LANES)
    dq = dq_ref[...].reshape(rows, LANES)
    k = k_ref[...].reshape(keys, LANES)
    v = v_ref[...].reshape(keys, LANES)
    dk = dk_ref[...].reshape(keys, LANES)
    dv = dv_ref[...].reshape(keys, LANES)
    kk = jnp.concatenate([k, dk], axis=-1)
    vv = jnp.concatenate([v, dv], axis=-1)
    lane = lax.broadcasted_iota(jnp.int32, (1, LANES), 1)
    low = lane < HEAD_DIM
    results = []
    for head in range(2):
        scale = jnp.where(low == (head == 0), HEAD_DIM ** -0.5, 0.0).astype(BF16)
        qh = q * scale
        dqh = dq * scale
        s = dot_t(qh, k)
        ds = dot_t(jnp.concatenate([dqh, qh], axis=-1), kk)
        p, dp = soft_parts(s, ds)
        both = dot(p, vv)
        results.append((both[:, :LANES], both[:, LANES:] + dot(dp, v)))
    shape = out_ref.shape[:1] + out_ref.shape[3:]
    for i in range(2):
        value = jnp.where(low, results[0][i], results[1][i]).astype(BF16)
        out_ref[:, i, 0] = value.reshape(shape)


def spatial(x, blocks=2):
    sources, _, frames, tokens, _ = x.shape
    per = sources // blocks

    def q_spec(a):
        return pl.BlockSpec((per, 1, 1, tokens, LANES), lambda f, b: (b, a, f, 0, 0))

    def k_spec(a):
        return pl.BlockSpec((sources, 1, 1, tokens, LANES), lambda f, b: (0, a, f, 0, 0))

    return pl.pallas_call(
        spatial_kernel,
        grid=(frames, blocks),
        in_specs=[q_spec(0), q_spec(3), k_spec(1), k_spec(2), k_spec(4), k_spec(5)],
        out_specs=pl.BlockSpec((per, 2, 1, tokens, LANES), lambda f, b: (b, 0, f, 0, 0)),
        out_shape=jax.ShapeDtypeStruct((sources, 2, frames, tokens, LANES), BF16),
        compiler_params=params(),
        cost_estimate=pl.CostEstimate(flops=9 << 30, bytes_accessed=4 << 20, transcendentals=4 << 20),
        name="spatial",
    )(*([x] * 6))


def temporal_kernel(x_ref, out_ref):
    sources = x_ref.shape[0]
    parts = sources // 8
    r_out = lax.broadcasted_iota(jnp.int32, (256, 256), 0)
    r_in = lax.broadcasted_iota(jnp.int32, (256, 256), 1)
    t_of, s_of, f_of = r_out // 16, (r_out % 16) // 2, r_out % 2
    gather = jnp.where(r_in == s_of * 32 + f_of * 16 + t_of, 1.0, 0.0).astype(BF16)
    t_at, s_at, f_at = r_in // 16, (r_in % 16) // 2, r_in % 2
    scatter = jnp.where(r_out == s_at * 32 + f_at * 16 + t_at, 1.0, 0.0).astype(BF16)
    members = []
    for a in range(6):
        members.append([x_ref[8 * i:8 * i + 8, a, 0].reshape(256, LANES) for i in range(parts)])
    moved = []
    for i in range(parts):
        rows = jnp.concatenate([members[a][i] for a in range(6)], axis=-1)
        moved.append(dot(gather, rows).astype(BF16))
    lane = lax.broadcasted_iota(jnp.int32, (1, LANES), 1)
    low = lane < HEAD_DIM
    scale0 = jnp.where(low, HEAD_DIM ** -0.5, 0.0).astype(BF16)
    scale1 = jnp.where(low, 0.0, HEAD_DIM ** -0.5).astype(BF16)
    row = lax.broadcasted_iota(jnp.int32, (256, LANES), 0)
    col = lax.broadcasted_iota(jnp.int32, (256, LANES), 1)
    same = ((row // 64) % 2) == (col // 64)
    pieces = [[], []]
    for g in range(8):
        tokens = (2 * g, 2 * g + 1)
        block = jnp.concatenate(
            [moved[i][t * 16:(t + 1) * 16] for t in tokens for i in range(parts)], axis=0)
        q, k, v, dq, dk, dv = [block[:, a * LANES:(a + 1) * LANES] for a in range(6)]
        qh = jnp.concatenate([q * scale0, q * scale1], axis=0)
        dqh = jnp.concatenate([dq * scale0, dq * scale1], axis=0)
        s = jnp.where(same, dot_t(qh, k), -jnp.inf)
        ds = dot_t(jnp.concatenate([dqh, qh], axis=-1), jnp.concatenate([k, dk], axis=-1))
        p, dp = soft_parts(s, ds)
        both = dot(p, jnp.concatenate([v, dv], axis=-1))
        o, do = both[:, :LANES], both[:, LANES:] + dot(dp, v)
        pieces[0].append(jnp.where(low, o[:LANES], o[LANES:]).astype(BF16))
        pieces[1].append(jnp.where(low, do[:LANES], do[LANES:]).astype(BF16))
    for i in range(parts):
        sides = []
        for side in range(2):
            sides.append(jnp.concatenate(
                [pieces[side][t // 2][(t % 2) * 64 + i * 16:(t % 2) * 64 + i * 16 + 16] for t in range(16)], axis=0))
        back = dot(scatter, jnp.concatenate(sides, axis=-1)).astype(BF16)
        for side in range(2):
            out_ref[8 * i:8 * i + 8, side, 0] = back[:, side * LANES:(side + 1) * LANES].reshape(8, 2, 16, LANES)


def temporal(x):
    sources, _, pairs, frames, tokens, _ = x.shape
    return pl.pallas_call(
        temporal_kernel,
        grid=(pairs,),
        in_specs=[pl.BlockSpec((sources, 6, 1, frames, tokens, LANES), lambda h: (0, 0, h, 0, 0, 0))],
        out_specs=pl.BlockSpec((sources, 2, 1, frames, tokens, LANES), lambda h: (0, 0, h, 0, 0, 0)),
        out_shape=jax.ShapeDtypeStruct((sources, 2, pairs, frames, tokens, LANES), BF16),
        compiler_params=params(),
        cost_estimate=pl.CostEstimate(flops=4 << 30, bytes_accessed=4 << 20, transcendentals=1 << 20),
        name="temporal",
    )(x)


def combine_kernel(s_ref, t_ref, out_ref, d_out_ref):
    groups = t_ref.shape[0]
    for i, ref in ((0, out_ref), (1, d_out_ref)):
        for pair in range(2):
            for f in range(2):
                for g in range(groups):
                    a = s_ref[pair, i, f, g * 16:(g + 1) * 16].astype(F32)
                    b = t_ref[g, 0, i, pair, f].astype(F32)
                    ref[f, g * 16:(g + 1) * 16, pair * LANES:(pair + 1) * LANES] = (a + b).astype(BF16)


def combine(s, t):
    pairs, _, frames, tokens, _ = s.shape
    groups, lane_groups = t.shape[:2]
    shape = jax.ShapeDtypeStruct((frames, tokens, pairs * LANES), BF16)
    spec = pl.BlockSpec((frames, tokens, 256), lambda d: (0, 0, d))
    return pl.pallas_call(
        combine_kernel,
        grid=(lane_groups,),
        in_specs=[
            pl.BlockSpec((2, 2, frames, tokens, LANES), lambda d: (d, 0, 0, 0, 0)),
            pl.BlockSpec((groups, 1, 2, 2, frames, 16, LANES), lambda d: (0, d, 0, 0, 0, 0, 0)),
        ],
        out_specs=[spec, spec],
        out_shape=[shape, shape],
        compiler_params=params(),
        cost_estimate=pl.CostEstimate(flops=0, bytes_accessed=3 << 20, transcendentals=0),
        name="combine",
    )(s, t)


def swap(x, axis):
    return lax.all_to_all(x, axis, split_axis=0, concat_axis=0, tiled=True)


def body(*arrays):
    space_in = swap(pack_space(arrays), "space")
    packed = pack_time(arrays)
    shape = packed.shape
    time_in = swap(packed.reshape((shape[0] * shape[1],) + shape[2:]), "tm")
    space_out = swap(spatial(space_in), "space")
    time_out = swap(temporal(time_in), "tm")
    return tuple(combine(space_out, time_out.reshape(shape[:2] + (2,) + shape[3:])))


def solution(mesh):
    spec = P("tm", "space", None)
    return jax.shard_map(
        body, mesh=mesh, in_specs=(spec,) * 6, out_specs=(spec,) * 2, check_vma=False)
```

time: 474 us -> 269 us (0.57); the launches traced: 465 us -> 268 us
  local copies, waits for them, and re-layouts: 94.3 us -> 7.92 us
  starting transfers between devices: 108 us -> 32.6 us
  waiting for transfers between devices: 191 us -> 148 us
  blocking collectives: 0 us -> 41.4 us
  other arithmetic: 40.9 us -> 0 us
  Pallas kernels: 0 us -> 37.5 us
  matrix products: 28.1 us -> 0 us
    all_to_all x16 -> x3, starting transfers between devices: 108 us -> 32.6 us  [swap(): return lax.all_to_all(x, axis, split_axis=0, concat_axis=0, tiled=True)]
    reshape x38 -> x0, local copies, waits for them, and re-layouts: 51.8 us -> none  [the longest x12 14.9 us: body(): member.reshape(frames_dev, time_count, tok_dev // time_count, width)]
    all_to_all x16 -> x3, waiting for transfers between devices: 191 us -> 148 us  [swap(): return lax.all_to_all(x, axis, split_axis=0, concat_axis=0, tiled=True)]
    all_to_all x0 -> x1, blocking collectives: none -> 41.4 us  [swap(): return lax.all_to_all(x, axis, split_axis=0, concat_axis=0, tiled=True)]
    pallas_call x0 -> x5, Pallas kernels: none -> 37.5 us  [the longest x1 15 us: spatial(): pl.pallas_call(spatial_kernel, grid=(frames, blocks), in_specs=[q_spec(0)...]
    dot_general x35 -> x0, matrix products: 25.8 us -> none  [the longest x9 10.2 us: attend(): jnp.dot(left_pair, right_pair.T, preferred_element_type=jnp.float32)]
    sub x1 -> x0, other arithmetic: 22.5 us -> none  [attend(): tangent - jnp.sum(probabilities * tangent, axis=-1, keepdims=True)]
    convert_element_type x14 -> x0, other arithmetic: 13.1 us -> none  [the longest x8 5.65 us: attend(): d_low = d_probabilities.astype(jnp.bfloat16)]
  transfers between devices with their start and end apart: 16 -> 3, of which waited for: 14 -> 3; matrix products, arithmetic and copies ran while one was open for 33% -> 0% of each run, Pallas kernels for 0% -> 11%
where the time goes in v1:
time: 269 us; the launch traced here: 268 us
  waiting for transfers between devices  148 us (55%)
  blocking collectives  41.4 us (15%)
  Pallas kernels  37.5 us (14%)
  starting transfers between devices  32.6 us (12%)
  local copies, waits for them, and re-layouts  7.92 us (3%)
    all_to_all x3, waiting for transfers between devices, swap(): return lax.all_to_all(x, axis, split_axis=0, concat_axis=0, tiled=True)  148 us
    all_to_all x1, blocking collectives, swap(): return lax.all_to_all(x, axis, split_axis=0, concat_axis=0, tiled=True)  41.4 us
    all_to_all x3, starting transfers between devices, swap(): return lax.all_to_all(x, axis, split_axis=0, concat_axis=0, tiled=True)  32.6 us
    pallas_call x1, Pallas kernels, spatial(): pl.pallas_call(spatial_kernel, grid=(frames, blocks), in_specs=[q_spec(0)...  15 us
    pallas_call x1, Pallas kernels, temporal(): pl.pallas_call(temporal_kernel, grid=(pairs,), in_specs=[pl.BlockSpec((so...  9.72 us
    unnamed x26, local copies, waits for them, and re-layouts  7.92 us
    pallas_call x1, Pallas kernels, pack_space(): pl.pallas_call(pack_space_kernel, grid=(pairs,), in_specs=[pl.BlockSpec((...  6.19 us
  transfers between devices with their start and end apart: 3, of which 3 were waited for; matrix products, arithmetic and copies ran while one was open for 0% of the time, Pallas kernels for 11%

profile of v1, /device:TPU:1, one launch (start us, length us, event | category | flops | bytes accessed | tf_op | source)
XLA Modules:
  0.0 268.4 jit_solution(7714930718439884574)
XLA Ops:
  0.6 0.0 copy-start
  0.6 1.0 copy-done
  1.7 0.0 copy-start.2
  1.7 1.0 copy-done.2
  2.7 0.0 copy-start.4
  2.7 1.0 copy-done.4
  3.8 0.0 copy-start.6
  3.8 1.0 copy-done.6
  4.8 0.0 copy-start.8
  4.8 1.0 copy-done.8
  5.8 1.0 copy-done.10
  6.9 6.2 %pack_space.1 = bf16[16,6,2,64,128]{4,3,2,1,0:T(8,128)(2,1)} custom-call(bf16[2,64,2048]{2,1,0:T(8,128)(2,1)S(1)} %copy-done, bf16[2,64,2048]{2,1,0:T(8,128)(2,1)S(1)} %copy-done.2, bf16[2,64,2048]{2,1,0:T(8,128)(2,1)S(1)} %copy-done.4, bf16[2,64,2048]{2,1,0:T(8,128)(2,1)S(1)} %copy-done.6, bf16[2,64,2048]{2,1,0:T(8,128)(2,1)S(1)} %copy-done.8, ...), custom_call_target="tpu_custom_call" | custom-call | bytes 6291456 | tf_op jit(solution)/shard_map/pack_space/pallas_call | solution.py:37
  13.1 0.0 copy-start.9
  13.1 0.0 copy-start.11
  13.1 10.7 %all-to-all-start = ((bf16[16,6,2,64,128]{4,3,2,1,0:T(8,128)(2,1)}), bf16[16,6,2,64,128]{4,3,2,1,0:T(8,128)(2,1)}, u32[]{:S(2)}, u32[]{:S(2)}) async-start(bf16[16,6,2,64,128]{4,3,2,1,0:T(8,128)(2,1)} %pack_space.1), calls=%async_computation | async-start | bytes 6291456 | tf_op jit(solution)/shard_map/all_to_all | solution.py:226
  23.8 0.0 copy-done.1
  23.8 0.0 copy-done.3
  23.8 0.0 copy-done.5
  23.8 0.0 copy-done.7
  23.9 0.0 copy-done.9
  23.9 0.0 copy-done.11
  23.9 3.9 %pack_time.1 = bf16[4,8,6,2,2,16,128]{6,5,4,3,2,1,0:T(8,128)(2,1)} custom-call(bf16[2,64,2048]{2,1,0:T(8,128)(2,1)S(1)} %copy-done.1, bf16[2,64,2048]{2,1,0:T(8,128)(2,1)S(1)} %copy-done.3, bf16[2,64,2048]{2,1,0:T(8,128)(2,1)S(1)} %copy-done.5, bf16[2,64,2048]{2,1,0:T(8,128)(2,1)S(1)} %copy-done.7, bf16[2,64,2048]{2,1,0:T(8,128)(2,1)S(1)} %copy-done.9, ...), custom_call_target="tpu_custom_call" | custom-call | bytes 6291456 | tf_op jit(solution)/shard_map/pack_time/pallas_call | solution.py:62
  27.8 70.0 %all-to-all-done.q_ref.dq_ref.k_ref.v_ref.dk_ref.dv_ref = bf16[16,6,2,64,128]{4,3,2,1,0:T(8,128)(2,1)} async-done(((bf16[16,6,2,64,128]{4,3,2,1,0:T(8,128)(2,1)}), bf16[16,6,2,64,128]{4,3,2,1,0:T(8,128)(2,1)}, u32[]{:S(2)}, u32[]{:S(2)}) %all-to-all-start) | async-done | bytes 3145760 | tf_op jit(solution)/shard_map/all_to_all | solution.py:226
  97.7 14.7 %all-to-all-start.2 = ((bf16[32,6,2,2,16,128]{5,4,3,2,1,0:T(8,128)(2,1)}), bf16[32,6,2,2,16,128]{5,4,3,2,1,0:T(8,128)(2,1)S(1)}, u32[]{:S(2)}, u32[]{:S(2)}) async-start(bf16[32,6,2,2,16,128]{5,4,3,2,1,0:T(8,128)(2,1)} %bitcast.3), calls=%async_computation.2 | async-start | bytes 6291456 | tf_op jit(solution)/shard_map/all_to_all | solution.py:226
  112.5 15.0 %spatial.1 = bf16[16,2,2,64,128]{4,3,2,1,0:T(8,128)(2,1)} custom-call(bf16[16,6,2,64,128]{4,3,2,1,0:T(8,128)(2,1)} %all-to-all-done.q_ref.dq_ref.k_ref.v_ref.dk_ref.dv_ref, bf16[16,6,2,64,128]{4,3,2,1,0:T(8,128)(2,1)} %all-to-all-done.q_ref.dq_ref.k_ref.v_ref.dk_ref.dv_ref, bf16[16,6,2,64,128]{4,3,2,1,0:T(8,128)(2,1)} %all-to-all-done.q_ref.dq_ref.k_ref.v_ref.dk_ref.dv_ref, ...), custom_call_target="tpu_custom_call" | custom-call | flops 9663676416 | bytes 4194304 | tf_op jit(solution)/shard_map/spatial/pallas_call | solution.py:120
  127.4 61.0 %all-to-all-done.2.x_ref = bf16[32,6,2,2,16,128]{5,4,3,2,1,0:T(8,128)(2,1)S(1)} async-done(((bf16[32,6,2,2,16,128]{5,4,3,2,1,0:T(8,128)(2,1)}), bf16[32,6,2,2,16,128]{5,4,3,2,1,0:T(8,128)(2,1)S(1)}, u32[]{:S(2)}, u32[]{:S(2)}) %all-to-all-start.2) | async-done | bytes 3145760 | tf_op jit(solution)/shard_map/all_to_all | solution.py:226
  188.4 1.6 copy-done.12
  190.1 7.2 %all-to-all-start.1 = ((bf16[16,2,2,64,128]{4,3,2,1,0:T(8,128)(2,1)}), bf16[16,2,2,64,128]{4,3,2,1,0:T(8,128)(2,1)S(1)}, u32[]{:S(2)}, u32[]{:S(2)}) async-start(bf16[16,2,2,64,128]{4,3,2,1,0:T(8,128)(2,1)} %spatial.1), calls=%async_computation.1 | async-start | bytes 2097152 | tf_op jit(solution)/shard_map/all_to_all | solution.py:226
  197.3 9.7 %temporal.1 = bf16[32,2,2,2,16,128]{5,4,3,2,1,0:T(8,128)(2,1)S(1)} custom-call(bf16[32,6,2,2,16,128]{5,4,3,2,1,0:T(8,128)(2,1)} %copy-done.12), custom_call_target="tpu_custom_call" | custom-call | flops 4294967296 | bytes 4194304 | tf_op jit(solution)/shard_map/temporal/pallas_call | solution.py:182
  207.0 17.2 %all-to-all-done.1.s_ref = bf16[16,2,2,64,128]{4,3,2,1,0:T(8,128)(2,1)S(1)} async-done(((bf16[16,2,2,64,128]{4,3,2,1,0:T(8,128)(2,1)}), bf16[16,2,2,64,128]{4,3,2,1,0:T(8,128)(2,1)S(1)}, u32[]{:S(2)}, u32[]{:S(2)}) %all-to-all-start.1) | async-done | bytes 1048608 | tf_op jit(solution)/shard_map/all_to_all | solution.py:226
  224.2 41.4 %all_to_all.20 = bf16[32,2,2,2,16,128]{5,4,3,2,1,0:T(8,128)(2,1)S(1)} all-to-all(bf16[32,2,2,2,16,128]{5,4,3,2,1,0:T(8,128)(2,1)S(1)} %temporal.1), channel_id=1, replica_groups=mesh['tm'=32,'space'=16] {'tm'}, dimensions={0} | all-to-all | bytes 2097152 | tf_op jit(solution)/shard_map/all_to_all | solution.py:226
  265.6 2.8 %combine.1 = (bf16[2,64,2048]{2,1,0:T(8,128)(2,1)}, bf16[2,64,2048]{2,1,0:T(8,128)(2,1)}) custom-call(bf16[16,2,2,64,128]{4,3,2,1,0:T(8,128)(2,1)S(1)} %all-to-all-done.1.s_ref, bf16[4,8,2,2,2,16,128]{6,5,4,3,2,1,0:T(8,128)(2,1)S(1)} %bitcast.2), custom_call_target="tpu_custom_call" | custom-call | bytes 3145728 | tf_op jit(solution)/shard_map/combine/pallas_call | solution.py:210
  (6 shorter events, 0.0 us)
Async XLA Ops:
  0.6 1.0 copy-start
  1.7 1.0 copy-start.2
  2.7 1.0 copy-start.4
  3.8 1.0 copy-start.6
  4.8 1.0 copy-start.8
  5.8 1.0 copy-start.10
  13.1 10.7 %copy-start.1 = (bf16[2,64,2048]{2,1,0:T(8,128)(2,1)S(1)}, bf16[2,64,2048]{2,1,0:T(8,128)(2,1)}, u32[]{:S(2)}) copy-start(bf16[2,64,2048]{2,1,0:T(8,128)(2,1)} %refs_0_.3) | copy-start | bytes 1572868
  13.1 10.8 %copy-start.3 = (bf16[2,64,2048]{2,1,0:T(8,128)(2,1)S(1)}, bf16[2,64,2048]{2,1,0:T(8,128)(2,1)}, u32[]{:S(2)}) copy-start(bf16[2,64,2048]{2,1,0:T(8,128)(2,1)} %refs_1_.3) | copy-start | bytes 1572868
  13.1 10.8 %copy-start.5 = (bf16[2,64,2048]{2,1,0:T(8,128)(2,1)S(1)}, bf16[2,64,2048]{2,1,0:T(8,128)(2,1)}, u32[]{:S(2)}) copy-start(bf16[2,64,2048]{2,1,0:T(8,128)(2,1)} %refs_2_.3) | copy-start | bytes 1572868
  13.1 10.8 %copy-start.7 = (bf16[2,64,2048]{2,1,0:T(8,128)(2,1)S(1)}, bf16[2,64,2048]{2,1,0:T(8,128)(2,1)}, u32[]{:S(2)}) copy-start(bf16[2,64,2048]{2,1,0:T(8,128)(2,1)} %refs_3_.3) | copy-start | bytes 1572868
  13.1 10.8 %copy-start.9 = (bf16[2,64,2048]{2,1,0:T(8,128)(2,1)S(1)}, bf16[2,64,2048]{2,1,0:T(8,128)(2,1)}, u32[]{:S(2)}) copy-start(bf16[2,64,2048]{2,1,0:T(8,128)(2,1)} %refs_4_.3) | copy-start | bytes 1572868
  13.1 10.8 %copy-start.11 = (bf16[2,64,2048]{2,1,0:T(8,128)(2,1)S(1)}, bf16[2,64,2048]{2,1,0:T(8,128)(2,1)}, u32[]{:S(2)}) copy-start(bf16[2,64,2048]{2,1,0:T(8,128)(2,1)} %refs_5_.3) | copy-start | bytes 1572868
  13.1 84.6 %all-to-all-start = ((bf16[16,6,2,64,128]{4,3,2,1,0:T(8,128)(2,1)}), bf16[16,6,2,64,128]{4,3,2,1,0:T(8,128)(2,1)}, u32[]{:S(2)}, u32[]{:S(2)}) async-start(bf16[16,6,2,64,128]{4,3,2,1,0:T(8,128)(2,1)} %pack_space.1), calls=%async_computation | async-start | bytes 6291456 | tf_op jit(solution)/shard_map/all_to_all | solution.py:226
  97.7 90.7 %all-to-all-start.2 = ((bf16[32,6,2,2,16,128]{5,4,3,2,1,0:T(8,128)(2,1)}), bf16[32,6,2,2,16,128]{5,4,3,2,1,0:T(8,128)(2,1)S(1)}, u32[]{:S(2)}, u32[]{:S(2)}) async-start(bf16[32,6,2,2,16,128]{5,4,3,2,1,0:T(8,128)(2,1)} %bitcast.3), calls=%async_computation.2 | async-start | bytes 6291456 | tf_op jit(solution)/shard_map/all_to_all | solution.py:226
  188.4 1.6 copy-start.12
  190.1 34.1 %all-to-all-start.1 = ((bf16[16,2,2,64,128]{4,3,2,1,0:T(8,128)(2,1)}), bf16[16,2,2,64,128]{4,3,2,1,0:T(8,128)(2,1)S(1)}, u32[]{:S(2)}, u32[]{:S(2)}) async-start(bf16[16,2,2,64,128]{4,3,2,1,0:T(8,128)(2,1)} %spatial.1), calls=%async_computation.1 | async-start | bytes 2097152 | tf_op jit(solution)/shard_map/all_to_all | solution.py:226

commit v2 on v0

v2 whole, which is shorter than its diff:
```python
import jax
import jax.numpy as jnp
import numpy as np
from jax import lax
from jax.experimental import pallas as pl
from jax.experimental.pallas import tpu as pltpu
from jax.sharding import PartitionSpec as P

HEAD_DIM = 64
LANES = 128
F32 = jnp.float32
BF16 = jnp.bfloat16
VMEM_LIMIT = 50 * 1024 * 1024
COST = pl.CostEstimate(flops=0, bytes_accessed=1024, transcendentals=0)


def dot_t(a, b):
    return lax.dot_general(a, b, (((1,), (1,)), ((), ())), preferred_element_type=F32)


def dot(a, b):
    return jnp.dot(a, b, preferred_element_type=F32)


MESH = (8, 2, 2, 4, 4)
AXES = ("tm", "space")
ROW = (64, LANES)


def groups_of(kind, core):
    ids = np.arange(512).reshape(MESH)[:, :, core]
    if kind == "space":
        found = [ids[y, zh].reshape(-1) for y in range(8) for zh in range(2)]
    elif kind == "time":
        found = [ids[:, :, x, z].reshape(-1) for x in range(4) for z in range(4)]
    else:
        found = [np.stack([ids[:, 0, x, z], ids[:, 1, x, z ^ 3]], axis=1).reshape(-1)
                 for x in range(4) for z in range(4)]
    return [[int(i) for i in group] for group in found]


def exchange(value, first, second):
    return lax.all_to_all(
        value, AXES, split_axis=0, concat_axis=0, tiled=True,
        axis_index_groups=groups_of(first, 0) + groups_of(second, 1))


def swap_cores(value):
    ids = np.arange(512).reshape(MESH)
    pairs = zip(ids.reshape(-1), ids[:, :, ::-1].reshape(-1))
    return lax.ppermute(value, AXES, [(int(a), int(b)) for a, b in pairs])


def call(kernel, scalars, operands, grid, in_specs, out_specs, out_shape, name, **kwargs):
    return pl.pallas_call(
        kernel,
        grid_spec=pltpu.PrefetchScalarGridSpec(
            num_scalar_prefetch=1, grid=grid, in_specs=in_specs, out_specs=out_specs),
        out_shape=out_shape,
        cost_estimate=COST,
        name=name,
        **kwargs,
    )(scalars, *operands)


def out_like(*shape):
    return jax.ShapeDtypeStruct(shape, BF16)


def swap_lanes():
    row = lax.broadcasted_iota(jnp.int32, (256, 256), 0)
    col = lax.broadcasted_iota(jnp.int32, (256, 256), 1)
    block = col // 64
    source = jnp.where(block == 1, col + 64, jnp.where(block == 2, col - 64, col))
    return jnp.where(row == source, 1.0, 0.0).astype(BF16)


def shift_lanes(down):
    row = lax.broadcasted_iota(jnp.int32, (LANES, LANES), 0)
    col = lax.broadcasted_iota(jnp.int32, (LANES, LANES), 1)
    return jnp.where(row == col + (64 if down else -64), 1.0, 0.0).astype(BF16)


def pack_rows(s, refs, out):
    swap = swap_lanes()
    rows = [
        jnp.concatenate(
            [refs[m][:, :, pair * LANES:(pair + 1) * LANES].reshape(128, LANES) for m in members], axis=-1)
        for pair in range(2) for members in ((3, 0), (1, 4), (2, 5))]
    rows = dot(jnp.concatenate(rows, axis=0), swap).astype(BF16)
    for pair in range(2):
        for a in range(3):
            for half in range(2):
                out[(2 * pair + half) ^ s[1], a] = (
                    rows[(3 * pair + a) * 128:(3 * pair + a + 1) * 128, half * LANES:(half + 1) * LANES]
                    .reshape(2, 64, LANES))


def pack_own(scalars, arrays):
    def kernel(s, *refs):
        pack_rows(s, refs[:6], refs[6])

    return call(
        kernel, scalars, arrays, (4,),
        [pl.BlockSpec((2, 64, 256), lambda n, s: (0, 0, 4 * s[0] + n))] * 6,
        pl.BlockSpec((4, 3, 2) + ROW, lambda n, s: (n, 0, 0, 0, 0)),
        out_like(16, 3, 4, *ROW), "pack_own")


def pack_other(scalars, own, other):
    def kernel(s, *refs):
        pack_rows(s, refs[:6], refs[7])

    def spec(a):
        return pl.BlockSpec((None, 2, 64, 256), lambda n, s: (a, 0, 0, n))

    return call(
        kernel, scalars, [other] * 6 + [own], (4,),
        [spec(a) for a in range(6)] + [pl.BlockSpec(memory_space=pl.ANY)],
        pl.BlockSpec((4, 3, 2) + ROW, lambda n, s: (n, 0, 1, 0, 0)),
        out_like(*own.shape), "pack_other", input_output_aliases={7: 0})


def other_heads(scalars, arrays):
    def kernel(s, *refs):
        for a in range(6):
            refs[6][a] = refs[a][...]

    return call(
        kernel, scalars, arrays, (2,),
        [pl.BlockSpec((2, 64, 512), lambda n, s: (0, 0, 2 * (1 - s[0]) + n))] * 6,
        pl.BlockSpec((6, 2, 64, 512), lambda n, s: (0, 0, 0, n)),
        out_like(6, 2, 64, 1024), "other_heads")


def choose(scalars, first, second):
    def kernel(s, first_ref, second_ref, out_ref):
        @pl.when(s[0] == 0)
        def _():
            out_ref[...] = first_ref[...]

        @pl.when(s[0] == 1)
        def _():
            out_ref[...] = second_ref[...]

    block = (4, 3, 4) + ROW
    return call(
        kernel, scalars, [first, second], (4,),
        [pl.BlockSpec(block, lambda n, s: (n * (1 - s[0]), 0, 0, 0, 0)),
         pl.BlockSpec(block, lambda n, s: (n * s[0], 0, 0, 0, 0))],
        pl.BlockSpec(block, lambda n, s: (n, 0, 0, 0, 0)),
        out_like(*first.shape), "choose")


def soft_parts(s, ds):
    e = jnp.exp(s - jnp.max(s, axis=-1, keepdims=True))
    p = e * (1.0 / jnp.sum(e, axis=-1, keepdims=True))
    dp = p * (ds - jnp.sum(p * ds, axis=-1, keepdims=True))
    return p.astype(BF16), dp.astype(BF16)


def spatial_kernel(x_ref, out_ref, q_both, q_low, values):
    block = pl.program_id(1)
    count = q_both.shape[0]

    @pl.when(block == 0)
    def _():
        q = x_ref[:, 0, 0].reshape(count, LANES) * BF16(HEAD_DIM ** -0.5)
        v = x_ref[:, 2, 0].reshape(count, LANES)
        q_both[...] = q
        q_low[...] = dot(q, shift_lanes(True)).astype(BF16)
        values[:count] = v
        values[count:] = dot(v, shift_lanes(False)).astype(BF16)

    rows = count // 2
    here = pl.ds(pl.multiple_of(block * rows, rows), rows)
    keys = x_ref[:, 1, 0].reshape(count, LANES)
    s = dot_t(q_low[here, :], keys)
    ds = dot_t(q_both[here, :], keys)
    found = dot(jnp.concatenate(soft_parts(s, ds), axis=-1), values[...]).astype(BF16)
    out_ref[:, 0] = found.reshape(8, 64, LANES)


def spatial(x):
    rows = pltpu.VMEM((1024, LANES), BF16)
    return pl.pallas_call(
        spatial_kernel,
        grid=(4, 2),
        in_specs=[pl.BlockSpec((16, 3, 1) + ROW, lambda f, b: (0, 0, f, 0, 0))],
        out_specs=pl.BlockSpec((8, 1) + ROW, lambda f, b: (b, f, 0, 0)),
        out_shape=out_like(16, 4, *ROW),
        scratch_shapes=[rows, rows, pltpu.VMEM((2048, LANES), BF16)],
        compiler_params=pltpu.CompilerParams(vmem_limit_bytes=VMEM_LIMIT),
        cost_estimate=COST,
        name="spatial",
    )(x)


def temporal_kernel(x_ref, out_ref):
    row = lax.broadcasted_iota(jnp.int32, (256, 256), 0)
    col = lax.broadcasted_iota(jnp.int32, (256, 256), 1)
    turn = jnp.where(col == (row % 16) * 16 + row // 16, 1.0, 0.0).astype(BF16)
    down, up = shift_lanes(True), shift_lanes(False)
    moved = []
    for i in range(4):
        rows = jnp.concatenate([x_ref[4 * i:4 * i + 4, a].reshape(256, LANES) for a in range(3)], axis=-1)
        rows = dot(turn, rows).astype(BF16)
        q, k, v = [rows[:, a * LANES:(a + 1) * LANES] for a in range(3)]
        q = q * BF16(HEAD_DIM ** -0.5)
        moved.append((q, dot(q, down).astype(BF16), k, v, dot(v, up).astype(BF16)))
    row = lax.broadcasted_iota(jnp.int32, (LANES, LANES), 0)
    col = lax.broadcasted_iota(jnp.int32, (LANES, LANES), 1)
    same = (row // 64) == (col // 64)
    pieces = []
    for g in range(8):
        q, q_low, k, v, v_up = [
            jnp.concatenate(
                [moved[i][m][t * 16:(t + 1) * 16] for t in (2 * g, 2 * g + 1) for i in range(4)], axis=0)
            for m in range(5)]
        scores = dot_t(jnp.concatenate([q_low, q], axis=0), k)
        p, dp = soft_parts(jnp.where(same, scores[:LANES], -jnp.inf), scores[LANES:])
        found = dot(jnp.concatenate([p, dp], axis=-1), jnp.concatenate([v, v_up], axis=0))
        pieces.append(found.astype(BF16))
    back = []
    for i in range(4):
        back.append(jnp.concatenate(
            [pieces[t // 2][(t % 2) * 64 + i * 16:(t % 2) * 64 + i * 16 + 16] for t in range(16)], axis=0))
    back = dot(turn, jnp.concatenate(back, axis=-1)).astype(BF16)
    for i in range(4):
        out_ref[4 * i:4 * i + 4] = back[:, i * LANES:(i + 1) * LANES].reshape(4, 4, 16, LANES)


def temporal(x):
    return pl.pallas_call(
        temporal_kernel,
        grid=(4,),
        in_specs=[pl.BlockSpec((16, 3, 4, 16, LANES), lambda t: (0, 0, 0, t, 0))],
        out_specs=pl.BlockSpec((16, 4, 16, LANES), lambda t: (0, 0, t, 0)),
        out_shape=out_like(16, 4, *ROW),
        compiler_params=pltpu.CompilerParams(vmem_limit_bytes=VMEM_LIMIT),
        cost_estimate=COST,
        name="temporal",
    )(x)


def add_round(a, b):
    return (a.astype(F32) + b.astype(F32)).astype(BF16)


def add_in_plane(scalars, plane, value, extra, frames, *after):
    def kernel(s, value_ref, extra_ref, *refs):
        out_ref = refs[-1]
        both = add_round(value_ref[...], extra_ref[...])
        out_ref[...] = jnp.where(s[0] == plane, both, value_ref[...])

    block = (8, 4 if frames is None else 2) + ROW
    spec = pl.BlockSpec(block, lambda n, s: (n, frames or 0, 0, 0))
    return call(
        kernel, scalars, [value, extra, *after], (2,),
        [spec, spec] + [pl.BlockSpec(memory_space=pl.ANY)] * len(after),
        pl.BlockSpec(block, lambda n, s: (n, 0, 0, 0)), out_like(16, *block[1:]), "add_in_plane")


def finish(scalars, value, extra, other):
    def kernel(s, value_ref, extra_ref, other_ref, out_ref, d_out_ref):
        swap = swap_lanes()
        side = pl.program_id(0) // 2
        flip = jnp.where(side == 0, s[1], s[2])
        rows = []
        for pair in range(4):
            halves = []
            for half in range(2):
                d = (2 * pair + half) ^ flip
                own = value_ref[d].reshape(128, LANES)
                own = jnp.where(s[0] == 1, add_round(own, extra_ref[d].reshape(128, LANES)), own)
                halves.append(jnp.where(side == 0, own, other_ref[d].reshape(128, LANES)))
            rows.append(jnp.concatenate(halves, axis=-1))
        rows = dot(jnp.concatenate(rows, axis=0), swap).astype(BF16)
        for pair in range(4):
            for i, ref in ((0, out_ref), (1, d_out_ref)):
                ref[:, :, pair * LANES:(pair + 1) * LANES] = (
                    rows[128 * pair:128 * pair + 128, i * LANES:(i + 1) * LANES].reshape(2, 64, LANES))

    block = (8, 2) + ROW
    own = pl.BlockSpec(block, lambda n, s: (jnp.minimum(n, 1), 0, 0, 0))
    result = pl.BlockSpec((2, 64, 512), lambda n, s: (0, 0, 2 * ((n // 2) ^ s[0]) + n % 2))
    return call(
        kernel, scalars, [value, extra, other], (4,),
        [own, own, pl.BlockSpec(block, lambda n, s: (jnp.maximum(n - 2, 0), 0, 0, 0))],
        [result, result], [out_like(2, 64, 2048)] * 2, "finish")


def body(*arrays):
    arrays = list(arrays)
    time = lax.axis_index("tm")
    core, zh3 = time % 2, 3 * ((time // 2) % 2)
    scalars = jnp.stack([core, zh3 * (1 - core), zh3 * core]).astype(jnp.int32)
    other = swap_cores(other_heads(scalars, arrays))
    packed = pack_other(scalars, pack_own(scalars, arrays), other)
    first = exchange(packed, "space", "time")
    chosen, passed = lax.optimization_barrier((choose(scalars, first, packed), swap_cores(first[0, 0, 0, :16])))
    second = exchange(chosen, "mirrored", "space")
    early = lax.cond(core == 0, spatial, temporal, first)
    in_time = lax.cond(core == 0, lambda x, done: temporal(x), lambda x, done: done, second, early)
    in_space = lax.cond(core == 0, lambda x, done: done, lambda x, done: spatial(x), second, early)
    third = exchange(in_time, "mirrored", "time")
    fourth = exchange(add_in_plane(scalars, 0, in_space, third, None, passed), "space", "space")
    other = swap_cores(add_in_plane(scalars, 1, fourth, third, 1))
    return tuple(finish(scalars, fourth, third, other))


def solution(mesh):
    spec = P("tm", "space", None)
    return jax.shard_map(
        body, mesh=mesh, in_specs=(spec,) * 6, out_specs=(spec,) * 2, check_vma=False)
```

time: 474 us -> 259 us (0.55); the launches traced: 465 us -> 258 us
  waiting for transfers between devices: 191 us -> 35 us
  blocking collectives: 0 us -> 104 us
  local copies, waits for them, and re-layouts: 94.3 us -> 5.84 us
  Pallas kernels: 0 us -> 57.9 us
  starting transfers between devices: 108 us -> 54.1 us
  other arithmetic: 40.9 us -> 0.67 us
  matrix products: 28.1 us -> 0 us
    all_to_all x16 -> x2, waiting for transfers between devices: 191 us -> 33.2 us  [exchange(): lax.all_to_all(value, AXES, split_axis=0, concat_axis=0, tiled=True, axis...]
    all_to_all x0 -> x2, blocking collectives: none -> 104 us  [exchange(): lax.all_to_all(value, AXES, split_axis=0, concat_axis=0, tiled=True, axis...]
    all_to_all x16 -> x2, starting transfers between devices: 108 us -> 14.7 us  [exchange(): lax.all_to_all(value, AXES, split_axis=0, concat_axis=0, tiled=True, axis...]
    pallas_call x0 -> x9, Pallas kernels: none -> 57.9 us  [the longest x7 28.1 us: call(): pl.pallas_call(kernel, grid_spec=pltpu.PrefetchScalarGridSpec(num_scalar_...]
    reshape x38 -> x0, local copies, waits for them, and re-layouts: 51.8 us -> none  [the longest x12 14.9 us: body(): member.reshape(frames_dev, time_count, tok_dev // time_count, width)]
    ppermute x0 -> x3, starting transfers between devices: none -> 39.4 us  [swap_cores(): return lax.ppermute(value, AXES, [(int(a), int(b)) for a, b in pairs])]
    dot_general x35 -> x0, matrix products: 25.8 us -> none  [the longest x9 10.2 us: attend(): jnp.dot(left_pair, right_pair.T, preferred_element_type=jnp.float32)]
    sub x1 -> x0, other arithmetic: 22.5 us -> none  [attend(): tangent - jnp.sum(probabilities * tangent, axis=-1, keepdims=True)]
  transfers between devices with their start and end apart: 16 -> 5, of which waited for: 14 -> 3; matrix products, arithmetic and copies ran while one was open for 33% -> 0% of each run, Pallas kernels for 0% -> 15%
where the time goes in v2:
time: 259 us; the launch traced here: 258 us
  blocking collectives  104 us (40%)
  Pallas kernels  57.9 us (22%)
  starting transfers between devices  54.1 us (21%)
  waiting for transfers between devices  35 us (14%)
  local copies, waits for them, and re-layouts  5.84 us (2%)
    all_to_all x2, blocking collectives, exchange(): lax.all_to_all(value, AXES, split_axis=0, concat_axis=0, tiled=True, axis...  104 us
    ppermute x3, starting transfers between devices, swap_cores(): return lax.ppermute(value, AXES, [(int(a), int(b)) for a, b in pairs])  39.4 us
    all_to_all x2, waiting for transfers between devices, exchange(): lax.all_to_all(value, AXES, split_axis=0, concat_axis=0, tiled=True, axis...  33.2 us
    pallas_call x7, Pallas kernels, call(): pl.pallas_call(kernel, grid_spec=pltpu.PrefetchScalarGridSpec(num_scalar_...  28.1 us
    pallas_call x1, Pallas kernels, spatial(): pl.pallas_call(spatial_kernel, grid=(4, 2), in_specs=[pl.BlockSpec((16, 3...  21 us
    all_to_all x2, starting transfers between devices, exchange(): lax.all_to_all(value, AXES, split_axis=0, concat_axis=0, tiled=True, axis...  14.7 us
    pallas_call x1, Pallas kernels, temporal(): pl.pallas_call(temporal_kernel, grid=(4,), in_specs=[pl.BlockSpec((16, 3,...  8.82 us
  transfers between devices with their start and end apart: 5, of which 3 were waited for; matrix products, arithmetic and copies ran while one was open for 0% of the time, Pallas kernels for 15%

profile of v2, /device:TPU:1, one launch (start us, length us, event | category | flops | bytes accessed | tf_op | source)
XLA Modules:
  0.0 258.0 jit_solution(17181742264070068863)
XLA Ops:
  0.7 0.7 pad_add_fusion.s
  1.3 3.1 %other_heads.1 = bf16[6,2,64,1024]{3,2,1,0:T(8,128)(2,1)} custom-call(s32[3]{0:T(128)} %pad_add_fusion.s, bf16[2,64,2048]{2,1,0:T(8,128)(2,1)} %refs_0_.3, bf16[2,64,2048]{2,1,0:T(8,128)(2,1)} %refs_1_.3, bf16[2,64,2048]{2,1,0:T(8,128)(2,1)} %refs_2_.3, bf16[2,64,2048]{2,1,0:T(8,128)(2,1)} %refs_3_.3, bf16[2,64,2048]{2,1,0:T(8,128)(2,1)} %refs_4_.3, ...), custom_call_target="tpu_custom_call" | custom-call | bytes 1024 | tf_op jit(solution)/shard_map/other_heads/pallas_call | solution.py:55
  4.5 8.8 %collective-permute-start = (bf16[6,2,64,1024]{3,2,1,0:T(8,128)(2,1)}, bf16[6,2,64,1024]{3,2,1,0:T(8,128)(2,1)S(1)}, u32[]{:S(2)}, u32[]{:S(2)}) collective-permute-start(bf16[6,2,64,1024]{3,2,1,0:T(8,128)(2,1)} %other_heads.1), channel_id=1, source_target_pairs={{0,16},{1,17},{2,18},{3,19},{4,20},{5,21},{6,22},{7,23},{8,24},{9,... | collective-permute-start | bytes 4718600 | tf_op jit(solution)/shard_map/ppermute | solution.py:51
  13.2 4.8 %pack_own.1.refs_6_ = bf16[16,3,4,64,128]{4,3,2,1,0:T(8,128)(2,1)} custom-call(s32[3]{0:T(128)} %pad_add_fusion.s, bf16[2,64,2048]{2,1,0:T(8,128)(2,1)} %refs_0_.3, bf16[2,64,2048]{2,1,0:T(8,128)(2,1)} %refs_1_.3, bf16[2,64,2048]{2,1,0:T(8,128)(2,1)} %refs_2_.3, bf16[2,64,2048]{2,1,0:T(8,128)(2,1)} %refs_3_.3, bf16[2,64,2048]{2,1,0:T(8,128)(2,1)} %refs_4_.3, ...), custom_call_target="tpu_custom_call" | custom-call | bytes 1024 | tf_op jit(solution)/shard_map/pack_own/pallas_call | solution.py:55
  18.0 0.0 collective-permute-done.refs_0_.refs_1_.refs_2_.refs_3_.refs_4_.refs_5_
  18.0 0.0 copy-start
  18.0 1.2 copy-done
  19.2 4.8 %pack_other.1.second_ref = bf16[16,3,4,64,128]{4,3,2,1,0:T(8,128)(2,1)} custom-call(s32[3]{0:T(128)} %pad_add_fusion.s, bf16[6,2,64,1024]{3,2,1,0:T(8,128)(2,1)} %copy-done, bf16[6,2,64,1024]{3,2,1,0:T(8,128)(2,1)} %copy-done, bf16[6,2,64,1024]{3,2,1,0:T(8,128)(2,1)} %copy-done, bf16[6,2,64,1024]{3,2,1,0:T(8,128)(2,1)} %copy-done, ...), custom_call_target="tpu_custom_call", output_to_operand_aliasing={{}: (7, {})} | custom-call | bytes 1024 | tf_op jit(solution)/shard_map/pack_other/pallas_call | solution.py:55
  24.0 54.3 %all_to_all.32.first_ref = bf16[16,3,4,64,128]{4,3,2,1,0:T(8,128)(2,1)S(1)} all-to-all(bf16[16,3,4,64,128]{4,3,2,1,0:T(8,128)(2,1)} %pack_other.1.second_ref), channel_id=1, replica_groups={{0,1,2,3,4,5,6,7,8,9,10,11,12,13,14,15},{32,33,34,35,36,37,38,39,40,41,..., dimensions={0} | all-to-all | bytes 6291456 | tf_op jit(solution)/shard_map/all_to_all | solution.py:43
  78.3 27.0 %collective-permute-start.1 = (bf16[16,128]{1,0:T(8,128)(2,1)S(1)}, bf16[16,128]{1,0:T(8,128)(2,1)S(1)}, u32[]{:S(2)}, u32[]{:S(2)}) collective-permute-start(bf16[16,128]{1,0:T(8,128)(2,1)S(1)} %slice_bitcast_fusion), channel_id=1, source_target_pairs={{0,16},{1,17},{2,18},{3,19},{4,20},{5,21},{6,22},{7,23},{8,24},{9,... | collective-permute-start | bytes 12296 | tf_op jit(solution)/shard_map/ppermute | solution.py:51
  105.3 4.9 %choose.1 = bf16[16,3,4,64,128]{4,3,2,1,0:T(8,128)(2,1)} custom-call(s32[3]{0:T(128)} %pad_add_fusion.s, bf16[16,3,4,64,128]{4,3,2,1,0:T(8,128)(2,1)S(1)} %all_to_all.32.first_ref, bf16[16,3,4,64,128]{4,3,2,1,0:T(8,128)(2,1)} %pack_other.1.second_ref), custom_call_target="tpu_custom_call" | custom-call | bytes 1024 | tf_op jit(solution)/shard_map/choose/pallas_call | solution.py:55
  110.2 0.0 collective-permute-done.1.refs_0_
  110.2 0.0 copy-start.3
  110.2 0.6 copy-done.3
  110.8 4.5 %all-to-all-start.1 = ((bf16[16,3,4,64,128]{4,3,2,1,0:T(8,128)(2,1)}), bf16[16,3,4,64,128]{4,3,2,1,0:T(8,128)(2,1)}, u32[]{:S(2)}, u32[]{:S(2)}) async-start(bf16[16,3,4,64,128]{4,3,2,1,0:T(8,128)(2,1)} %choose.1), calls=%async_computation.1 | async-start | bytes 6291456 | tf_op jit(solution)/shard_map/all_to_all | solution.py:43
  115.3 8.8 %conditional.3 = (bf16[16,4,64,128]{3,2,1,0:T(8,128)(2,1)}) conditional(s32[]{:T(128)} %convert_element_type.2, bf16[16,3,4,64,128]{4,3,2,1,0:T(8,128)(2,1)S(1)} %all_to_all.32.first_ref, bf16[16,3,4,64,128]{4,3,2,1,0:T(8,128)(2,1)S(1)} %all_to_all.32.first_ref), branch_computations={%region_0.1_spmd, %region_1.2_spmd} | conditional | bytes 1032 | solution.py:303
  115.3 8.8 %temporal.2 = bf16[16,4,64,128]{3,2,1,0:T(8,128)(2,1)} custom-call(bf16[16,3,4,64,128]{4,3,2,1,0:T(8,128)(2,1)S(1)} %x_ref), custom_call_target="tpu_custom_call" | custom-call | bytes 1024 | tf_op jit(solution)/shard_map/cond/branch_0_fun/temporal/pallas_call | solution.py:234
  124.1 33.2 %all-to-all-done.1 = bf16[16,3,4,64,128]{4,3,2,1,0:T(8,128)(2,1)} async-done(((bf16[16,3,4,64,128]{4,3,2,1,0:T(8,128)(2,1)}), bf16[16,3,4,64,128]{4,3,2,1,0:T(8,128)(2,1)}, u32[]{:S(2)}, u32[]{:S(2)}) %all-to-all-start.1) | async-done | bytes 3145760 | tf_op jit(solution)/shard_map/all_to_all | solution.py:43
  157.3 2.3 conditional.5
  157.3 2.3 copy.14
  159.6 10.2 %all-to-all-start.2 = ((bf16[16,4,64,128]{3,2,1,0:T(8,128)(2,1)}), bf16[16,4,64,128]{3,2,1,0:T(8,128)(2,1)S(1)}, u32[]{:S(2)}, u32[]{:S(2)}) async-start(bf16[16,4,64,128]{3,2,1,0:T(8,128)(2,1)} %get-tuple-element.23), calls=%async_computation.2 | async-start | bytes 2097152 | tf_op jit(solution)/shard_map/all_to_all | solution.py:43
  169.9 21.0 %conditional.4 = (bf16[16,4,64,128]{3,2,1,0:T(8,128)(2,1)}) conditional(s32[]{:T(128)} %convert_element_type.2, bf16[16,3,4,64,128]{4,3,2,1,0:T(8,128)(2,1)} %all-to-all-done.1, bf16[16,4,64,128]{3,2,1,0:T(8,128)(2,1)} %get-tuple-element.21), branch_computations={%region_2.3_spmd, %region_3.4_spmd} | conditional | bytes 1032 | solution.py:305
  169.9 21.0 %spatial.3 = bf16[16,4,64,128]{3,2,1,0:T(8,128)(2,1)} custom-call(bf16[16,3,4,64,128]{4,3,2,1,0:T(8,128)(2,1)} %x_ref.2), custom_call_target="tpu_custom_call" | custom-call | bytes 1024 | tf_op jit(solution)/shard_map/cond/branch_0_fun/spatial/pallas_call | solution.py:186
  190.9 0.1 all-to-all-done.2.extra_ref
  190.9 1.0 copy-done.1
  191.9 3.2 %add_in_plane.2 = bf16[16,4,64,128]{3,2,1,0:T(8,128)(2,1)} custom-call(s32[3]{0:T(128)} %pad_add_fusion.s, bf16[16,4,64,128]{3,2,1,0:T(8,128)(2,1)} %get-tuple-element.22.value_ref, bf16[16,4,64,128]{3,2,1,0:T(8,128)(2,1)} %copy-done.1, bf16[16,128]{1,0:T(8,128)(2,1)} %copy-done.3), custom_call_target="tpu_custom_call" | custom-call | bytes 1024 | tf_op jit(solution)/shard_map/add_in_plane/pallas_call | solution.py:55
  195.1 49.4 %all_to_all.33.value_ref = bf16[16,4,64,128]{3,2,1,0:T(8,128)(2,1)} all-to-all(bf16[16,4,64,128]{3,2,1,0:T(8,128)(2,1)} %add_in_plane.2), channel_id=1, replica_groups={{0,1,2,3,4,5,6,7,8,9,10,11,12,13,14,15},{32,33,34,35,36,37,38,39,40,41,..., dimensions={0} | all-to-all | bytes 2097152 | tf_op jit(solution)/shard_map/all_to_all | solution.py:43
  244.5 2.7 %add_in_plane.3 = bf16[16,2,64,128]{3,2,1,0:T(8,128)(2,1)} custom-call(s32[3]{0:T(128)} %pad_add_fusion.s, bf16[16,4,64,128]{3,2,1,0:T(8,128)(2,1)} %all_to_all.33.value_ref, bf16[16,4,64,128]{3,2,1,0:T(8,128)(2,1)} %copy-done.1), custom_call_target="tpu_custom_call" | custom-call | bytes 1024 | tf_op jit(solution)/shard_map/add_in_plane/pallas_call | solution.py:55
  247.2 3.6 %collective-permute-start.2 = (bf16[16,2,64,128]{3,2,1,0:T(8,128)(2,1)}, bf16[16,2,64,128]{3,2,1,0:T(8,128)(2,1)S(1)}, u32[]{:S(2)}, u32[]{:S(2)}) collective-permute-start(bf16[16,2,64,128]{3,2,1,0:T(8,128)(2,1)} %add_in_plane.3), channel_id=1, source_target_pairs={{0,16},{1,17},{2,18},{3,19},{4,20},{5,21},{6,22},{7,23},{8,24},{9,... | collective-permute-start | bytes 1572872 | tf_op jit(solution)/shard_map/ppermute | solution.py:51
  250.8 1.7 collective-permute-done.2.other_ref
  252.6 0.8 copy-done.2
  253.4 4.7 %finish.1 = (bf16[2,64,2048]{2,1,0:T(8,128)(2,1)}, bf16[2,64,2048]{2,1,0:T(8,128)(2,1)}) custom-call(s32[3]{0:T(128)} %pad_add_fusion.s, bf16[16,4,64,128]{3,2,1,0:T(8,128)(2,1)} %all_to_all.33.value_ref, bf16[16,4,64,128]{3,2,1,0:T(8,128)(2,1)} %copy-done.1, bf16[16,2,64,128]{3,2,1,0:T(8,128)(2,1)} %copy-done.2), custom_call_target="tpu_custom_call" | custom-call | bytes 1024 | tf_op jit(solution)/shard_map/finish/pallas_call | solution.py:55
  (3 shorter events, 0.0 us)
Async XLA Ops:
  4.5 13.6 %collective-permute-start = (bf16[6,2,64,1024]{3,2,1,0:T(8,128)(2,1)}, bf16[6,2,64,1024]{3,2,1,0:T(8,128)(2,1)S(1)}, u32[]{:S(2)}, u32[]{:S(2)}) collective-permute-start(bf16[6,2,64,1024]{3,2,1,0:T(8,128)(2,1)} %other_heads.1), channel_id=1, source_target_pairs={{0,16},{1,17},{2,18},{3,19},{4,20},{5,21},{6,22},{7,23},{8,24},{9,... | collective-permute-start | bytes 4718600 | tf_op jit(solution)/shard_map/ppermute | solution.py:51
  18.0 1.2 copy-start
  78.3 31.9 %collective-permute-start.1 = (bf16[16,128]{1,0:T(8,128)(2,1)S(1)}, bf16[16,128]{1,0:T(8,128)(2,1)S(1)}, u32[]{:S(2)}, u32[]{:S(2)}) collective-permute-start(bf16[16,128]{1,0:T(8,128)(2,1)S(1)} %slice_bitcast_fusion), channel_id=1, source_target_pairs={{0,16},{1,17},{2,18},{3,19},{4,20},{5,21},{6,22},{7,23},{8,24},{9,... | collective-permute-start | bytes 12296 | tf_op jit(solution)/shard_map/ppermute | solution.py:51
  110.2 0.6 copy-start.3
  110.8 46.5 %all-to-all-start.1 = ((bf16[16,3,4,64,128]{4,3,2,1,0:T(8,128)(2,1)}), bf16[16,3,4,64,128]{4,3,2,1,0:T(8,128)(2,1)}, u32[]{:S(2)}, u32[]{:S(2)}) async-start(bf16[16,3,4,64,128]{4,3,2,1,0:T(8,128)(2,1)} %choose.1), calls=%async_computation.1 | async-start | bytes 6291456 | tf_op jit(solution)/shard_map/all_to_all | solution.py:43
  159.6 31.3 %all-to-all-start.2 = ((bf16[16,4,64,128]{3,2,1,0:T(8,128)(2,1)}), bf16[16,4,64,128]{3,2,1,0:T(8,128)(2,1)S(1)}, u32[]{:S(2)}, u32[]{:S(2)}) async-start(bf16[16,4,64,128]{3,2,1,0:T(8,128)(2,1)} %get-tuple-element.23), calls=%async_computation.2 | async-start | bytes 2097152 | tf_op jit(solution)/shard_map/all_to_all | solution.py:43
  190.9 1.0 copy-start.1
  247.2 5.4 %collective-permute-start.2 = (bf16[16,2,64,128]{3,2,1,0:T(8,128)(2,1)}, bf16[16,2,64,128]{3,2,1,0:T(8,128)(2,1)S(1)}, u32[]{:S(2)}, u32[]{:S(2)}) collective-permute-start(bf16[16,2,64,128]{3,2,1,0:T(8,128)(2,1)} %add_in_plane.3), channel_id=1, source_target_pairs={{0,16},{1,17},{2,18},{3,19},{4,20},{5,21},{6,22},{7,23},{8,24},{9,... | collective-permute-start | bytes 1572872 | tf_op jit(solution)/shard_map/ppermute | solution.py:51
  252.6 0.8 copy-start.2

commit v3 on v2

--- a/solution.py
+++ b/solution.py
@@ -31,18 +31,16 @@
     ids = np.arange(512).reshape(MESH)[:, :, core]
     if kind == "space":
         found = [ids[y, zh].reshape(-1) for y in range(8) for zh in range(2)]
-    elif kind == "time":
-        found = [ids[:, :, x, z].reshape(-1) for x in range(4) for z in range(4)]
     else:
         found = [np.stack([ids[:, 0, x, z], ids[:, 1, x, z ^ 3]], axis=1).reshape(-1)
                  for x in range(4) for z in range(4)]
     return [[int(i) for i in group] for group in found]
 
 
-def exchange(value, first, second):
+def exchange(value, kind):
     return lax.all_to_all(
         value, AXES, split_axis=0, concat_axis=0, tiled=True,
-        axis_index_groups=groups_of(first, 0) + groups_of(second, 1))
+        axis_index_groups=groups_of(kind, 0) + groups_of(kind, 1))
 
 
 def swap_cores(value):
@@ -131,25 +129,6 @@
         [pl.BlockSpec((2, 64, 512), lambda n, s: (0, 0, 2 * (1 - s[0]) + n))] * 6,
         pl.BlockSpec((6, 2, 64, 512), lambda n, s: (0, 0, 0, n)),
         out_like(6, 2, 64, 1024), "other_heads")
-
-
-def choose(scalars, first, second):
-    def kernel(s, first_ref, second_ref, out_ref):
-        @pl.when(s[0] == 0)
-        def _():
-            out_ref[...] = first_ref[...]
-
-        @pl.when(s[0] == 1)
-        def _():
-            out_ref[...] = second_ref[...]
-
-    block = (4, 3, 4) + ROW
-    return call(
-        kernel, scalars, [first, second], (4,),
-        [pl.BlockSpec(block, lambda n, s: (n * (1 - s[0]), 0, 0, 0, 0)),
-         pl.BlockSpec(block, lambda n, s: (n * s[0], 0, 0, 0, 0))],
-        pl.BlockSpec(block, lambda n, s: (n, 0, 0, 0, 0)),
-        out_like(*first.shape), "choose")
 
 
 def soft_parts(s, ds):
@@ -247,33 +226,16 @@
     return (a.astype(F32) + b.astype(F32)).astype(BF16)
 
 
-def add_in_plane(scalars, plane, value, extra, frames, *after):
-    def kernel(s, value_ref, extra_ref, *refs):
-        out_ref = refs[-1]
-        both = add_round(value_ref[...], extra_ref[...])
-        out_ref[...] = jnp.where(s[0] == plane, both, value_ref[...])
-
-    block = (8, 4 if frames is None else 2) + ROW
-    spec = pl.BlockSpec(block, lambda n, s: (n, frames or 0, 0, 0))
-    return call(
-        kernel, scalars, [value, extra, *after], (2,),
-        [spec, spec] + [pl.BlockSpec(memory_space=pl.ANY)] * len(after),
-        pl.BlockSpec(block, lambda n, s: (n, 0, 0, 0)), out_like(16, *block[1:]), "add_in_plane")
-
-
-def finish(scalars, value, extra, other):
-    def kernel(s, value_ref, extra_ref, other_ref, out_ref, d_out_ref):
+def finish(scalars, value, other, after):
+    def kernel(s, value_ref, other_ref, after_ref, out_ref, d_out_ref):
         swap = swap_lanes()
         side = pl.program_id(0) // 2
-        flip = jnp.where(side == 0, s[1], s[2])
         rows = []
         for pair in range(4):
             halves = []
             for half in range(2):
-                d = (2 * pair + half) ^ flip
-                own = value_ref[d].reshape(128, LANES)
-                own = jnp.where(s[0] == 1, add_round(own, extra_ref[d].reshape(128, LANES)), own)
-                halves.append(jnp.where(side == 0, own, other_ref[d].reshape(128, LANES)))
+                d = (2 * pair + half) ^ s[1]
+                halves.append(jnp.where(side == 0, value_ref[d].reshape(128, LANES), other_ref[d].reshape(128, LANES)))
             rows.append(jnp.concatenate(halves, axis=-1))
         rows = dot(jnp.concatenate(rows, axis=0), swap).astype(BF16)
         for pair in range(4):
@@ -282,31 +244,33 @@
                     rows[128 * pair:128 * pair + 128, i * LANES:(i + 1) * LANES].reshape(2, 64, LANES))
 
     block = (8, 2) + ROW
-    own = pl.BlockSpec(block, lambda n, s: (jnp.minimum(n, 1), 0, 0, 0))
     result = pl.BlockSpec((2, 64, 512), lambda n, s: (0, 0, 2 * ((n // 2) ^ s[0]) + n % 2))
     return call(
-        kernel, scalars, [value, extra, other], (4,),
-        [own, own, pl.BlockSpec(block, lambda n, s: (jnp.maximum(n - 2, 0), 0, 0, 0))],
+        kernel, scalars, [value, other, after], (4,),
+        [pl.BlockSpec(block, lambda n, s: (jnp.minimum(n, 1), 0, 0, 0)),
+         pl.BlockSpec(block, lambda n, s: (jnp.maximum(n - 2, 0), 0, 0, 0)),
+         pl.BlockSpec(memory_space=pl.ANY)],
         [result, result], [out_like(2, 64, 2048)] * 2, "finish")
 
 
 def body(*arrays):
     arrays = list(arrays)
     time = lax.axis_index("tm")
-    core, zh3 = time % 2, 3 * ((time // 2) % 2)
-    scalars = jnp.stack([core, zh3 * (1 - core), zh3 * core]).astype(jnp.int32)
+    core = time % 2
+    scalars = jnp.stack([core, 3 * ((time // 2) % 2)]).astype(jnp.int32)
     other = swap_cores(other_heads(scalars, arrays))
     packed = pack_other(scalars, pack_own(scalars, arrays), other)
-    first = exchange(packed, "space", "time")
-    chosen, passed = lax.optimization_barrier((choose(scalars, first, packed), swap_cores(first[0, 0, 0, :16])))
-    second = exchange(chosen, "mirrored", "space")
-    early = lax.cond(core == 0, spatial, temporal, first)
-    in_time = lax.cond(core == 0, lambda x, done: temporal(x), lambda x, done: done, second, early)
-    in_space = lax.cond(core == 0, lambda x, done: done, lambda x, done: spatial(x), second, early)
-    third = exchange(in_time, "mirrored", "time")
-    fourth = exchange(add_in_plane(scalars, 0, in_space, third, None, passed), "space", "space")
-    other = swap_cores(add_in_plane(scalars, 1, fourth, third, 1))
-    return tuple(finish(scalars, fourth, third, other))
+
+    def to_space(x):
+        return exchange(x, "space")
+
+    tokens = lax.cond(core == 0, to_space, lambda x: x, packed)
+    tokens, passed = lax.optimization_barrier((tokens, swap_cores(tokens[0, 0, 0, :16])))
+    tokens = lax.cond(core == 1, to_space, lambda x: x, tokens)
+    in_space, times = lax.optimization_barrier((spatial(tokens), exchange(tokens, "mirrored")))
+    total = add_round(in_space, exchange(temporal(times), "mirrored"))
+    total = exchange(total, "space")
+    return tuple(finish(scalars, total, swap_cores(total[:, 2:]), passed))
 
 
 def solution(mesh):

time: 259 us -> 268 us (1.035)
  starting transfers between devices: 54.1 us -> 71.3 us
  Pallas kernels: 57.9 us -> 46.6 us
  waiting for transfers between devices: 35 us -> 44.7 us
  blocking collectives: 104 us -> 97.9 us
    ppermute x3, starting transfers between devices: 39.4 us -> 59.2 us  [swap_cores(): return lax.ppermute(value, AXES, [(int(a), int(b)) for a, b in pairs])]
    pallas_call x7 -> x4, Pallas kernels: 28.1 us -> 17.4 us  [call(): pl.pallas_call(kernel, grid_spec=pltpu.PrefetchScalarGridSpec(num_scalar_...]
    all_to_all x2 -> x1, waiting for transfers between devices: 33.2 us -> 42.1 us  [exchange(): lax.all_to_all(value, AXES, split_axis=0, concat_axis=0, tiled=True, axis...]
    all_to_all x2 -> x3, blocking collectives: 104 us -> 97.9 us  [exchange(): lax.all_to_all(value, AXES, split_axis=0, concat_axis=0, tiled=True, axis...]
    all_to_all x2 -> x1, starting transfers between devices: 14.7 us -> 12 us  [exchange(): lax.all_to_all(value, AXES, split_axis=0, concat_axis=0, tiled=True, axis...]
  transfers between devices with their start and end apart: 5 -> 4, of which waited for: 3 -> 3; matrix products, arithmetic and copies ran while one was open for 0% -> 0% of each run, Pallas kernels for 15% -> 9%
where the time goes in v3:
time: 268 us
  blocking collectives  97.9 us (37%)
  starting transfers between devices  71.3 us (27%)
  Pallas kernels  46.6 us (17%)
  waiting for transfers between devices  44.7 us (17%)
  local copies, waits for them, and re-layouts  5.2 us (2%)
    all_to_all x3, blocking collectives, exchange(): lax.all_to_all(value, AXES, split_axis=0, concat_axis=0, tiled=True, axis...  97.9 us
    ppermute x3, starting transfers between devices, swap_cores(): return lax.ppermute(value, AXES, [(int(a), int(b)) for a, b in pairs])  59.2 us
    all_to_all x1, waiting for transfers between devices, exchange(): lax.all_to_all(value, AXES, split_axis=0, concat_axis=0, tiled=True, axis...  42.1 us
    pallas_call x1, Pallas kernels, spatial(): pl.pallas_call(spatial_kernel, grid=(4, 2), in_specs=[pl.BlockSpec((16, 3...  20.4 us
    pallas_call x4, Pallas kernels, call(): pl.pallas_call(kernel, grid_spec=pltpu.PrefetchScalarGridSpec(num_scalar_...  17.4 us
    all_to_all x1, starting transfers between devices, exchange(): lax.all_to_all(value, AXES, split_axis=0, concat_axis=0, tiled=True, axis...  12 us
    pallas_call x1, Pallas kernels, temporal(): pl.pallas_call(temporal_kernel, grid=(4,), in_specs=[pl.BlockSpec((16, 3,...  8.84 us
  transfers between devices with their start and end apart: 4, of which 3 were waited for; matrix products, arithmetic and copies ran while one was open for 0% of the time, Pallas kernels for 9%

profile of v3, /device:TPU:1, one launch (start us, length us, event | category | flops | bytes accessed | tf_op | source)
XLA Modules:
  0.0 267.5 jit_solution(13746417369597620072)
XLA Ops:
  0.7 0.7 pad_add_fusion.s
  1.3 3.1 %other_heads.1 = bf16[6,2,64,1024]{3,2,1,0:T(8,128)(2,1)} custom-call(s32[2]{0:T(128)} %pad_add_fusion.s, bf16[2,64,2048]{2,1,0:T(8,128)(2,1)} %refs_0_.3, bf16[2,64,2048]{2,1,0:T(8,128)(2,1)} %refs_1_.3, bf16[2,64,2048]{2,1,0:T(8,128)(2,1)} %refs_2_.3, bf16[2,64,2048]{2,1,0:T(8,128)(2,1)} %refs_3_.3, bf16[2,64,2048]{2,1,0:T(8,128)(2,1)} %refs_4_.3, ...), custom_call_target="tpu_custom_call" | custom-call | bytes 1024 | tf_op jit(solution)/shard_map/other_heads/pallas_call | solution.py:53
  4.5 8.8 %collective-permute-start = (bf16[6,2,64,1024]{3,2,1,0:T(8,128)(2,1)}, bf16[6,2,64,1024]{3,2,1,0:T(8,128)(2,1)S(1)}, u32[]{:S(2)}, u32[]{:S(2)}) collective-permute-start(bf16[6,2,64,1024]{3,2,1,0:T(8,128)(2,1)} %other_heads.1), channel_id=1, source_target_pairs={{0,16},{1,17},{2,18},{3,19},{4,20},{5,21},{6,22},{7,23},{8,24},{9,... | collective-permute-start | bytes 4718600 | tf_op jit(solution)/shard_map/ppermute | solution.py:49
  13.2 4.8 %pack_own.1.refs_6_ = bf16[16,3,4,64,128]{4,3,2,1,0:T(8,128)(2,1)} custom-call(s32[2]{0:T(128)} %pad_add_fusion.s, bf16[2,64,2048]{2,1,0:T(8,128)(2,1)} %refs_0_.3, bf16[2,64,2048]{2,1,0:T(8,128)(2,1)} %refs_1_.3, bf16[2,64,2048]{2,1,0:T(8,128)(2,1)} %refs_2_.3, bf16[2,64,2048]{2,1,0:T(8,128)(2,1)} %refs_3_.3, bf16[2,64,2048]{2,1,0:T(8,128)(2,1)} %refs_4_.3, ...), custom_call_target="tpu_custom_call" | custom-call | bytes 1024 | tf_op jit(solution)/shard_map/pack_own/pallas_call | solution.py:53
  18.1 0.0 collective-permute-done.refs_0_.refs_1_.refs_2_.refs_3_.refs_4_.refs_5_
  18.1 0.0 copy-start
  18.1 1.1 copy-done
  19.2 4.8 %pack_other.1 = bf16[16,3,4,64,128]{4,3,2,1,0:T(8,128)(2,1)} custom-call(s32[2]{0:T(128)} %pad_add_fusion.s, bf16[6,2,64,1024]{3,2,1,0:T(8,128)(2,1)} %copy-done, bf16[6,2,64,1024]{3,2,1,0:T(8,128)(2,1)} %copy-done, bf16[6,2,64,1024]{3,2,1,0:T(8,128)(2,1)} %copy-done, bf16[6,2,64,1024]{3,2,1,0:T(8,128)(2,1)} %copy-done, ...), custom_call_target="tpu_custom_call", output_to_operand_aliasing={{}: (7, {})} | custom-call | bytes 1024 | tf_op jit(solution)/shard_map/pack_other/pallas_call | solution.py:53
  24.1 0.7 slice_bitcast_fusion
  24.7 48.5 %collective-permute-start.1 = (bf16[16,128]{1,0:T(8,128)(2,1)S(1)}, bf16[16,128]{1,0:T(8,128)(2,1)S(1)}, u32[]{:S(2)}, u32[]{:S(2)}) collective-permute-start(bf16[16,128]{1,0:T(8,128)(2,1)S(1)} %slice_bitcast_fusion), channel_id=1, source_target_pairs={{0,16},{1,17},{2,18},{3,19},{4,20},{5,21},{6,22},{7,23},{8,24},{9,... | collective-permute-start | bytes 12296 | tf_op jit(solution)/shard_map/ppermute | solution.py:49
  73.3 0.8 collective-permute-done.1.after_ref
  74.1 0.0 copy-start.3
  74.1 0.6 copy-done.3
  74.7 47.0 %conditional.3 = (bf16[16,3,4,64,128]{4,3,2,1,0:T(8,128)(2,1)}) conditional(s32[]{:T(128)} %convert_element_type.15, bf16[16,3,4,64,128]{4,3,2,1,0:T(8,128)(2,1)} %get-tuple-element.20, bf16[16,3,4,64,128]{4,3,2,1,0:T(8,128)(2,1)} %get-tuple-element.20), branch_computations={%region_2.3_spmd, %region_3.4_spmd} | conditional | bytes 12582920 | solution.py:269
  74.7 1.9 copy.15
  76.6 45.1 %all_to_all.24 = bf16[16,3,4,64,128]{4,3,2,1,0:T(8,128)(2,1)} all-to-all(bf16[16,3,4,64,128]{4,3,2,1,0:T(8,128)(2,1)S(1)} %copy.15), channel_id=1, replica_groups={{0,1,2,3,4,5,6,7,8,9,10,11,12,13,14,15},{32,33,34,35,36,37,38,39,40,41,..., dimensions={0} | all-to-all | bytes 6291456 | tf_op jit(solution)/shard_map/cond/branch_1_fun/all_to_all | solution.py:41
  121.6 12.0 %all-to-all-start.2 = ((bf16[16,3,4,64,128]{4,3,2,1,0:T(8,128)(2,1)}), bf16[16,3,4,64,128]{4,3,2,1,0:T(8,128)(2,1)}, u32[]{:S(2)}, u32[]{:S(2)}) async-start(bf16[16,3,4,64,128]{4,3,2,1,0:T(8,128)(2,1)} %get-tuple-element.21.x_ref), calls=%async_computation.2 | async-start | bytes 6291456 | tf_op jit(solution)/shard_map/all_to_all | solution.py:41
  133.7 20.4 %spatial.1 = bf16[16,4,64,128]{3,2,1,0:T(8,128)(2,1)S(1)} custom-call(bf16[16,3,4,64,128]{4,3,2,1,0:T(8,128)(2,1)} %get-tuple-element.21.x_ref), custom_call_target="tpu_custom_call" | custom-call | bytes 1024 | tf_op jit(solution)/shard_map/spatial/pallas_call | solution.py:165
  154.1 42.1 %all-to-all-done.2.x_ref = bf16[16,3,4,64,128]{4,3,2,1,0:T(8,128)(2,1)} async-done(((bf16[16,3,4,64,128]{4,3,2,1,0:T(8,128)(2,1)}), bf16[16,3,4,64,128]{4,3,2,1,0:T(8,128)(2,1)}, u32[]{:S(2)}, u32[]{:S(2)}) %all-to-all-start.2) | async-done | bytes 3145760 | tf_op jit(solution)/shard_map/all_to_all | solution.py:41
  196.2 8.8 %temporal.1 = bf16[16,4,64,128]{3,2,1,0:T(8,128)(2,1)S(1)} custom-call(bf16[16,3,4,64,128]{4,3,2,1,0:T(8,128)(2,1)} %all-to-all-done.2.x_ref), custom_call_target="tpu_custom_call" | custom-call | bytes 1024 | tf_op jit(solution)/shard_map/temporal/pallas_call | solution.py:213
  205.0 27.3 %all_to_all.25 = bf16[16,4,64,128]{3,2,1,0:T(8,128)(2,1)S(1)} all-to-all(bf16[16,4,64,128]{3,2,1,0:T(8,128)(2,1)S(1)} %temporal.1), channel_id=1, replica_groups={{0,35,64,99,128,163,192,227,256,291,320,355,384,419,448,483},{1,34,65,9..., dimensions={0} | all-to-all | bytes 2097152 | tf_op jit(solution)/shard_map/all_to_all | solution.py:41
  232.3 0.4 add_convert_fusion
  232.8 25.5 %all_to_all.26.value_ref = bf16[16,4,64,128]{3,2,1,0:T(8,128)(2,1)S(1)} all-to-all(bf16[16,4,64,128]{3,2,1,0:T(8,128)(2,1)S(1)} %add_convert_fusion), channel_id=1, replica_groups={{0,1,2,3,4,5,6,7,8,9,10,11,12,13,14,15},{32,33,34,35,36,37,38,39,40,41,..., dimensions={0} | all-to-all | bytes 2097152 | tf_op jit(solution)/shard_map/all_to_all | solution.py:41
  258.3 0.0 copy-start.1
  258.3 1.9 collective-permute-start.2
  260.3 1.9 collective-permute-done.2.other_ref
  262.1 0.0 copy-done.1
  262.1 0.0 copy-start.2
  262.1 0.8 copy-done.2
  263.0 4.6 %finish.1 = (bf16[2,64,2048]{2,1,0:T(8,128)(2,1)}, bf16[2,64,2048]{2,1,0:T(8,128)(2,1)}) custom-call(s32[2]{0:T(128)} %pad_add_fusion.s, bf16[16,4,64,128]{3,2,1,0:T(8,128)(2,1)} %copy-done.1, bf16[16,2,64,128]{3,2,1,0:T(8,128)(2,1)} %copy-done.2, bf16[16,128]{1,0:T(8,128)(2,1)} %copy-done.3), custom_call_target="tpu_custom_call" | custom-call | bytes 1024 | tf_op jit(solution)/shard_map/finish/pallas_call | solution.py:53
  (2 shorter events, 0.0 us)
Async XLA Ops:
  4.5 13.6 %collective-permute-start = (bf16[6,2,64,1024]{3,2,1,0:T(8,128)(2,1)}, bf16[6,2,64,1024]{3,2,1,0:T(8,128)(2,1)S(1)}, u32[]{:S(2)}, u32[]{:S(2)}) collective-permute-start(bf16[6,2,64,1024]{3,2,1,0:T(8,128)(2,1)} %other_heads.1), channel_id=1, source_target_pairs={{0,16},{1,17},{2,18},{3,19},{4,20},{5,21},{6,22},{7,23},{8,24},{9,... | collective-permute-start | bytes 4718600 | tf_op jit(solution)/shard_map/ppermute | solution.py:49
  18.1 1.2 copy-start
  24.7 49.3 %collective-permute-start.1 = (bf16[16,128]{1,0:T(8,128)(2,1)S(1)}, bf16[16,128]{1,0:T(8,128)(2,1)S(1)}, u32[]{:S(2)}, u32[]{:S(2)}) collective-permute-start(bf16[16,128]{1,0:T(8,128)(2,1)S(1)} %slice_bitcast_fusion), channel_id=1, source_target_pairs={{0,16},{1,17},{2,18},{3,19},{4,20},{5,21},{6,22},{7,23},{8,24},{9,... | collective-permute-start | bytes 12296 | tf_op jit(solution)/shard_map/ppermute | solution.py:49
  74.1 0.6 copy-start.3
  121.6 74.5 %all-to-all-start.2 = ((bf16[16,3,4,64,128]{4,3,2,1,0:T(8,128)(2,1)}), bf16[16,3,4,64,128]{4,3,2,1,0:T(8,128)(2,1)}, u32[]{:S(2)}, u32[]{:S(2)}) async-start(bf16[16,3,4,64,128]{4,3,2,1,0:T(8,128)(2,1)} %get-tuple-element.21.x_ref), calls=%async_computation.2 | async-start | bytes 6291456 | tf_op jit(solution)/shard_map/all_to_all | solution.py:41
  258.3 3.9 %copy-start.1 = (bf16[16,4,64,128]{3,2,1,0:T(8,128)(2,1)}, bf16[16,4,64,128]{3,2,1,0:T(8,128)(2,1)S(1)}, u32[]{:S(2)}) copy-start(bf16[16,4,64,128]{3,2,1,0:T(8,128)(2,1)S(1)} %all_to_all.26.value_ref) | copy-start | bytes 3145732
  258.3 3.8 %collective-permute-start.2 = (bf16[16,2,64,128]{3,2,1,0:T(8,128)(2,1)S(1)}, bf16[16,2,64,128]{3,2,1,0:T(8,128)(2,1)S(1)}, u32[]{:S(2)}, u32[]{:S(2)}) collective-permute-start(bf16[16,2,64,128]{3,2,1,0:T(8,128)(2,1)S(1)} %slice.9), channel_id=1, source_target_pairs={{0,16},{1,17},{2,18},{3,19},{4,20},{5,21},{6,22},{7,23},{8,24},{9,... | collective-permute-start | bytes 1572872 | tf_op jit(solution)/shard_map/ppermute | solution.py:49
  262.1 0.8 copy-start.2

commit v4 on v3

--- a/solution.py
+++ b/solution.py
@@ -138,37 +138,24 @@
     return p.astype(BF16), dp.astype(BF16)
 
 
-def spatial_kernel(x_ref, out_ref, q_both, q_low, values):
-    block = pl.program_id(1)
-    count = q_both.shape[0]
-
-    @pl.when(block == 0)
-    def _():
-        q = x_ref[:, 0, 0].reshape(count, LANES) * BF16(HEAD_DIM ** -0.5)
-        v = x_ref[:, 2, 0].reshape(count, LANES)
-        q_both[...] = q
-        q_low[...] = dot(q, shift_lanes(True)).astype(BF16)
-        values[:count] = v
-        values[count:] = dot(v, shift_lanes(False)).astype(BF16)
-
-    rows = count // 2
-    here = pl.ds(pl.multiple_of(block * rows, rows), rows)
-    keys = x_ref[:, 1, 0].reshape(count, LANES)
-    s = dot_t(q_low[here, :], keys)
-    ds = dot_t(q_both[here, :], keys)
-    found = dot(jnp.concatenate(soft_parts(s, ds), axis=-1), values[...]).astype(BF16)
-    out_ref[:, 0] = found.reshape(8, 64, LANES)
+def spatial_kernel(x_ref, out_ref):
+    q, keys, v = [x_ref[:, a, 0].reshape(1024, LANES) for a in range(3)]
+    q = q * BF16(HEAD_DIM ** -0.5)
+    q_low = dot(q, shift_lanes(True)).astype(BF16)
+    values = jnp.concatenate([v, dot(v, shift_lanes(False)).astype(BF16)], axis=0)
+    for block in range(2):
+        rows = slice(512 * block, 512 * block + 512)
+        both = jnp.concatenate(soft_parts(dot_t(q_low[rows], keys), dot_t(q[rows], keys)), axis=-1)
+        out_ref[8 * block:8 * block + 8, 0] = dot(both, values).astype(BF16).reshape(8, 64, LANES)
 
 
 def spatial(x):
-    rows = pltpu.VMEM((1024, LANES), BF16)
     return pl.pallas_call(
         spatial_kernel,
-        grid=(4, 2),
-        in_specs=[pl.BlockSpec((16, 3, 1) + ROW, lambda f, b: (0, 0, f, 0, 0))],
-        out_specs=pl.BlockSpec((8, 1) + ROW, lambda f, b: (b, f, 0, 0)),
+        grid=(4,),
+        in_specs=[pl.BlockSpec((16, 3, 1) + ROW, lambda f: (0, 0, f, 0, 0))],
+        out_specs=pl.BlockSpec((16, 1) + ROW, lambda f: (0, f, 0, 0)),
         out_shape=out_like(16, 4, *ROW),
-        scratch_shapes=[rows, rows, pltpu.VMEM((2048, LANES), BF16)],
         compiler_params=pltpu.CompilerParams(vmem_limit_bytes=VMEM_LIMIT),
         cost_estimate=COST,
         name="spatial",
@@ -267,8 +254,8 @@
     tokens = lax.cond(core == 0, to_space, lambda x: x, packed)
     tokens, passed = lax.optimization_barrier((tokens, swap_cores(tokens[0, 0, 0, :16])))
     tokens = lax.cond(core == 1, to_space, lambda x: x, tokens)
-    in_space, times = lax.optimization_barrier((spatial(tokens), exchange(tokens, "mirrored")))
-    total = add_round(in_space, exchange(temporal(times), "mirrored"))
+    in_time = temporal(exchange(tokens, "mirrored"))
+    total = add_round(spatial(tokens), exchange(in_time, "mirrored"))
     total = exchange(total, "space")
     return tuple(finish(scalars, total, swap_cores(total[:, 2:]), passed))
 

time: 268 us -> 252 us (0.940)
  blocking collectives: 97.9 us -> 138 us
  waiting for transfers between devices: 44.7 us -> 6.43 us
  starting transfers between devices: 71.3 us -> 62.1 us
  Pallas kernels: 46.6 us -> 40.4 us
  local copies, waits for them, and re-layouts: 5.2 us -> 2.28 us
    all_to_all x3, blocking collectives: 97.9 us -> 138 us  [exchange(): lax.all_to_all(value, AXES, split_axis=0, concat_axis=0, tiled=True, axis...]
    all_to_all x1, waiting for transfers between devices: 42.1 us -> 3.75 us  [exchange(): lax.all_to_all(value, AXES, split_axis=0, concat_axis=0, tiled=True, axis...]
    all_to_all x1, starting transfers between devices: 12 us -> 4.03 us  [exchange(): lax.all_to_all(value, AXES, split_axis=0, concat_axis=0, tiled=True, axis...]
    pallas_call x1, Pallas kernels: 20.4 us -> 15.7 us  [spatial(): pl.pallas_call(spatial_kernel, grid=(4,), in_specs=[pl.BlockSpec((16, 3,...]
  transfers between devices with their start and end apart: 4 -> 4, of which waited for: 3 -> 3; matrix products, arithmetic and copies ran while one was open for 0% -> 0% of each run, Pallas kernels for 9% -> 8%
where the time goes in v4:
time: 252 us; the launch traced here: 251 us
  blocking collectives  138 us (55%)
  starting transfers between devices  62.1 us (25%)
  Pallas kernels  40.4 us (16%)
  waiting for transfers between devices  6.43 us (3%)
    all_to_all x3, blocking collectives, exchange(): lax.all_to_all(value, AXES, split_axis=0, concat_axis=0, tiled=True, axis...  138 us
    ppermute x3, starting transfers between devices, swap_cores(): return lax.ppermute(value, AXES, [(int(a), int(b)) for a, b in pairs])  58.1 us
    pallas_call x1, Pallas kernels, spatial(): pl.pallas_call(spatial_kernel, grid=(4,), in_specs=[pl.BlockSpec((16, 3,...  15.7 us
    pallas_call x4, Pallas kernels, call(): pl.pallas_call(kernel, grid_spec=pltpu.PrefetchScalarGridSpec(num_scalar_...  15.2 us
    pallas_call x1, Pallas kernels, temporal(): pl.pallas_call(temporal_kernel, grid=(4,), in_specs=[pl.BlockSpec((16, 3,...  9.54 us
  transfers between devices with their start and end apart: 4, of which 3 were waited for; matrix products, arithmetic and copies ran while one was open for 0% of the time, Pallas kernels for 8%

profile of v4, /device:TPU:1, one launch (start us, length us, event | category | flops | bytes accessed | tf_op | source)
XLA Modules:
  0.0 251.3 jit_solution(11121529437298539594)
XLA Ops:
  0.7 0.6 pad_add_fusion.s
  1.2 3.2 %other_heads.1 = bf16[6,2,64,1024]{3,2,1,0:T(8,128)(2,1)} custom-call(s32[2]{0:T(128)} %pad_add_fusion.s, bf16[2,64,2048]{2,1,0:T(8,128)(2,1)} %refs_0_.3, bf16[2,64,2048]{2,1,0:T(8,128)(2,1)} %refs_1_.3, bf16[2,64,2048]{2,1,0:T(8,128)(2,1)} %refs_2_.3, bf16[2,64,2048]{2,1,0:T(8,128)(2,1)} %refs_3_.3, bf16[2,64,2048]{2,1,0:T(8,128)(2,1)} %refs_4_.3, ...), custom_call_target="tpu_custom_call" | custom-call | bytes 1024 | tf_op jit(solution)/shard_map/other_heads/pallas_call | solution.py:53
  4.4 8.8 %collective-permute-start = (bf16[6,2,64,1024]{3,2,1,0:T(8,128)(2,1)}, bf16[6,2,64,1024]{3,2,1,0:T(8,128)(2,1)}, u32[]{:S(2)}, u32[]{:S(2)}) collective-permute-start(bf16[6,2,64,1024]{3,2,1,0:T(8,128)(2,1)} %other_heads.1), channel_id=1, source_target_pairs={{0,16},{1,17},{2,18},{3,19},{4,20},{5,21},{6,22},{7,23},{8,24},{9,... | collective-permute-start | bytes 4718600 | tf_op jit(solution)/shard_map/ppermute | solution.py:49
  13.2 3.8 %pack_own.1.refs_6_ = bf16[16,3,4,64,128]{4,3,2,1,0:T(8,128)(2,1)S(1)} custom-call(s32[2]{0:T(128)} %pad_add_fusion.s, bf16[2,64,2048]{2,1,0:T(8,128)(2,1)} %refs_0_.3, bf16[2,64,2048]{2,1,0:T(8,128)(2,1)} %refs_1_.3, bf16[2,64,2048]{2,1,0:T(8,128)(2,1)} %refs_2_.3, bf16[2,64,2048]{2,1,0:T(8,128)(2,1)} %refs_3_.3, bf16[2,64,2048]{2,1,0:T(8,128)(2,1)} %refs_4_.3, ...), custom_call_target="tpu_custom_call" | custom-call | bytes 1024 | tf_op jit(solution)/shard_map/pack_own/pallas_call | solution.py:53
  17.0 0.0 collective-permute-done.refs_0_.refs_1_.refs_2_.refs_3_.refs_4_.refs_5_
  17.0 3.7 %pack_other.1 = bf16[16,3,4,64,128]{4,3,2,1,0:T(8,128)(2,1)S(1)} custom-call(s32[2]{0:T(128)} %pad_add_fusion.s, bf16[6,2,64,1024]{3,2,1,0:T(8,128)(2,1)} %collective-permute-done.refs_0_.refs_1_.refs_2_.refs_3_.refs_4_.refs_5_, ...), custom_call_target="tpu_custom_call", output_to_operand_aliasing={{}: (7, {})} | custom-call | bytes 1024 | tf_op jit(solution)/shard_map/pack_other/pallas_call | solution.py:53
  20.7 47.4 %collective-permute-start.1 = (bf16[16,128]{1,0:T(8,128)(2,1)S(1)}, bf16[16,128]{1,0:T(8,128)(2,1)S(1)}, u32[]{:S(2)}, u32[]{:S(2)}) collective-permute-start(bf16[16,128]{1,0:T(8,128)(2,1)S(1)} %slice_bitcast_fusion), channel_id=1, source_target_pairs={{0,16},{1,17},{2,18},{3,19},{4,20},{5,21},{6,22},{7,23},{8,24},{9,... | collective-permute-start | bytes 12296 | tf_op jit(solution)/shard_map/ppermute | solution.py:49
  68.1 0.8 collective-permute-done.1.after_ref
  68.9 0.0 copy-start.3
  68.9 0.6 copy-done.3
  69.5 49.6 %conditional.3 = (bf16[16,3,4,64,128]{4,3,2,1,0:T(8,128)(2,1)S(1)}) conditional(s32[]{:T(128)} %convert_element_type.15, bf16[16,3,4,64,128]{4,3,2,1,0:T(8,128)(2,1)S(1)} %get-tuple-element.16, bf16[16,3,4,64,128]{4,3,2,1,0:T(8,128)(2,1)S(1)} %get-tuple-element.16), branch_computations={%region_2.3_spmd, %region_3.4_spmd} | conditional | bytes 12582920 | solution.py:256
  69.5 0.8 copy.15
  70.3 48.8 %all_to_all.24 = bf16[16,3,4,64,128]{4,3,2,1,0:T(8,128)(2,1)S(1)} all-to-all(bf16[16,3,4,64,128]{4,3,2,1,0:T(8,128)(2,1)S(1)} %copy.15), channel_id=1, replica_groups={{0,1,2,3,4,5,6,7,8,9,10,11,12,13,14,15},{32,33,34,35,36,37,38,39,40,41,..., dimensions={0} | all-to-all | bytes 6291456 | tf_op jit(solution)/shard_map/cond/branch_1_fun/all_to_all | solution.py:41
  119.0 0.0 copy-start
  119.1 65.2 %all_to_all.25.x_ref = bf16[16,3,4,64,128]{4,3,2,1,0:T(8,128)(2,1)} all-to-all(bf16[16,3,4,64,128]{4,3,2,1,0:T(8,128)(2,1)S(1)} %get-tuple-element.17.x_ref), channel_id=1, replica_groups={{0,35,64,99,128,163,192,227,256,291,320,355,384,419,448,483},{1,34,65,9..., dimensions={0} | all-to-all | bytes 6291456 | tf_op jit(solution)/shard_map/all_to_all | solution.py:41
  184.2 0.0 copy-done
  184.2 9.5 %temporal.1 = bf16[16,4,64,128]{3,2,1,0:T(8,128)(2,1)} custom-call(bf16[16,3,4,64,128]{4,3,2,1,0:T(8,128)(2,1)} %all_to_all.25.x_ref), custom_call_target="tpu_custom_call" | custom-call | bytes 1024 | tf_op jit(solution)/shard_map/temporal/pallas_call | solution.py:200
  193.7 4.0 %all-to-all-start.3 = ((bf16[16,4,64,128]{3,2,1,0:T(8,128)(2,1)}), bf16[16,4,64,128]{3,2,1,0:T(8,128)(2,1)S(1)}, u32[]{:S(2)}, u32[]{:S(2)}) async-start(bf16[16,4,64,128]{3,2,1,0:T(8,128)(2,1)} %temporal.1), calls=%async_computation.3 | async-start | bytes 2097152 | tf_op jit(solution)/shard_map/all_to_all | solution.py:41
  197.8 15.7 %spatial.1 = bf16[16,4,64,128]{3,2,1,0:T(8,128)(2,1)S(1)} custom-call(bf16[16,3,4,64,128]{4,3,2,1,0:T(8,128)(2,1)} %copy-done), custom_call_target="tpu_custom_call" | custom-call | bytes 1024 | tf_op jit(solution)/shard_map/spatial/pallas_call | solution.py:153
  213.5 3.8 %all-to-all-done.3 = bf16[16,4,64,128]{3,2,1,0:T(8,128)(2,1)S(1)} async-done(((bf16[16,4,64,128]{3,2,1,0:T(8,128)(2,1)}), bf16[16,4,64,128]{3,2,1,0:T(8,128)(2,1)S(1)}, u32[]{:S(2)}, u32[]{:S(2)}) %all-to-all-start.3) | async-done | bytes 1048608 | tf_op jit(solution)/shard_map/all_to_all | solution.py:41
  217.2 0.4 add_convert_fusion
  217.6 24.4 %all_to_all.26.value_ref = bf16[16,4,64,128]{3,2,1,0:T(8,128)(2,1)S(1)} all-to-all(bf16[16,4,64,128]{3,2,1,0:T(8,128)(2,1)S(1)} %add_convert_fusion), channel_id=1, replica_groups={{0,1,2,3,4,5,6,7,8,9,10,11,12,13,14,15},{32,33,34,35,36,37,38,39,40,41,..., dimensions={0} | all-to-all | bytes 2097152 | tf_op jit(solution)/shard_map/all_to_all | solution.py:41
  242.0 0.0 copy-start.1
  242.1 1.9 collective-permute-start.2
  244.0 1.9 collective-permute-done.2.other_ref
  245.9 0.0 copy-done.1
  245.9 0.0 copy-start.2
  245.9 0.8 copy-done.2
  246.7 4.6 %finish.1 = (bf16[2,64,2048]{2,1,0:T(8,128)(2,1)}, bf16[2,64,2048]{2,1,0:T(8,128)(2,1)}) custom-call(s32[2]{0:T(128)} %pad_add_fusion.s, bf16[16,4,64,128]{3,2,1,0:T(8,128)(2,1)} %copy-done.1, bf16[16,2,64,128]{3,2,1,0:T(8,128)(2,1)} %copy-done.2, bf16[16,128]{1,0:T(8,128)(2,1)} %copy-done.3), custom_call_target="tpu_custom_call" | custom-call | bytes 1024 | tf_op jit(solution)/shard_map/finish/pallas_call | solution.py:53
  (3 shorter events, 0.1 us)
Async XLA Ops:
  4.4 12.6 %collective-permute-start = (bf16[6,2,64,1024]{3,2,1,0:T(8,128)(2,1)}, bf16[6,2,64,1024]{3,2,1,0:T(8,128)(2,1)}, u32[]{:S(2)}, u32[]{:S(2)}) collective-permute-start(bf16[6,2,64,1024]{3,2,1,0:T(8,128)(2,1)} %other_heads.1), channel_id=1, source_target_pairs={{0,16},{1,17},{2,18},{3,19},{4,20},{5,21},{6,22},{7,23},{8,24},{9,... | collective-permute-start | bytes 4718600 | tf_op jit(solution)/shard_map/ppermute | solution.py:49
  20.7 48.2 %collective-permute-start.1 = (bf16[16,128]{1,0:T(8,128)(2,1)S(1)}, bf16[16,128]{1,0:T(8,128)(2,1)S(1)}, u32[]{:S(2)}, u32[]{:S(2)}) collective-permute-start(bf16[16,128]{1,0:T(8,128)(2,1)S(1)} %slice_bitcast_fusion), channel_id=1, source_target_pairs={{0,16},{1,17},{2,18},{3,19},{4,20},{5,21},{6,22},{7,23},{8,24},{9,... | collective-permute-start | bytes 12296 | tf_op jit(solution)/shard_map/ppermute | solution.py:49
  68.9 0.6 copy-start.3
  119.0 65.2 %copy-start = (bf16[16,3,4,64,128]{4,3,2,1,0:T(8,128)(2,1)}, bf16[16,3,4,64,128]{4,3,2,1,0:T(8,128)(2,1)S(1)}, u32[]{:S(2)}) copy-start(bf16[16,3,4,64,128]{4,3,2,1,0:T(8,128)(2,1)S(1)} %get-tuple-element.17.x_ref) | copy-start | bytes 9437188
  193.7 23.5 %all-to-all-start.3 = ((bf16[16,4,64,128]{3,2,1,0:T(8,128)(2,1)}), bf16[16,4,64,128]{3,2,1,0:T(8,128)(2,1)S(1)}, u32[]{:S(2)}, u32[]{:S(2)}) async-start(bf16[16,4,64,128]{3,2,1,0:T(8,128)(2,1)} %temporal.1), calls=%async_computation.3 | async-start | bytes 2097152 | tf_op jit(solution)/shard_map/all_to_all | solution.py:41
  242.0 3.9 %copy-start.1 = (bf16[16,4,64,128]{3,2,1,0:T(8,128)(2,1)}, bf16[16,4,64,128]{3,2,1,0:T(8,128)(2,1)S(1)}, u32[]{:S(2)}) copy-start(bf16[16,4,64,128]{3,2,1,0:T(8,128)(2,1)S(1)} %all_to_all.26.value_ref) | copy-start | bytes 3145732
  242.1 3.8 %collective-permute-start.2 = (bf16[16,2,64,128]{3,2,1,0:T(8,128)(2,1)S(1)}, bf16[16,2,64,128]{3,2,1,0:T(8,128)(2,1)S(1)}, u32[]{:S(2)}, u32[]{:S(2)}) collective-permute-start(bf16[16,2,64,128]{3,2,1,0:T(8,128)(2,1)S(1)} %slice.9), channel_id=1, source_target_pairs={{0,16},{1,17},{2,18},{3,19},{4,20},{5,21},{6,22},{7,23},{8,24},{9,... | collective-permute-start | bytes 1572872 | tf_op jit(solution)/shard_map/ppermute | solution.py:49
  245.9 0.8 copy-start.2

commit v5 on v4

--- a/solution.py
+++ b/solution.py
@@ -31,6 +31,8 @@
     ids = np.arange(512).reshape(MESH)[:, :, core]
     if kind == "space":
         found = [ids[y, zh].reshape(-1) for y in range(8) for zh in range(2)]
+    elif kind == "time":
+        found = [ids[:, :, x, z].reshape(-1) for x in range(4) for z in range(4)]
     else:
         found = [np.stack([ids[:, 0, x, z], ids[:, 1, x, z ^ 3]], axis=1).reshape(-1)
                  for x in range(4) for z in range(4)]
@@ -217,11 +219,12 @@
     def kernel(s, value_ref, other_ref, after_ref, out_ref, d_out_ref):
         swap = swap_lanes()
         side = pl.program_id(0) // 2
+        flip = jnp.where(side == 0, s[1], s[2])
         rows = []
         for pair in range(4):
             halves = []
             for half in range(2):
-                d = (2 * pair + half) ^ s[1]
+                d = (2 * pair + half) ^ flip
                 halves.append(jnp.where(side == 0, value_ref[d].reshape(128, LANES), other_ref[d].reshape(128, LANES)))
             rows.append(jnp.concatenate(halves, axis=-1))
         rows = dot(jnp.concatenate(rows, axis=0), swap).astype(BF16)
@@ -243,20 +246,29 @@
 def body(*arrays):
     arrays = list(arrays)
     time = lax.axis_index("tm")
-    core = time % 2
-    scalars = jnp.stack([core, 3 * ((time // 2) % 2)]).astype(jnp.int32)
+    core, zh3 = time % 2, 3 * ((time // 2) % 2)
+    scalars = jnp.stack([core, zh3 * (1 - core), zh3 * core]).astype(jnp.int32)
     other = swap_cores(other_heads(scalars, arrays))
     packed = pack_other(scalars, pack_own(scalars, arrays), other)
 
-    def to_space(x):
-        return exchange(x, "space")
-
-    tokens = lax.cond(core == 0, to_space, lambda x: x, packed)
+    def lead(x):
+        return exchange(x, "space"), jnp.zeros((16, 4) + ROW, BF16)
+
+    def follow(x):
+        return x, temporal(exchange(x, "time"))
+
+    def lead_rest(x, _):
+        found = exchange(temporal(exchange(x, "mirrored")), "mirrored")
+        return exchange(add_round(spatial(x), found), "space")
+
+    def follow_rest(x, in_time):
+        x = exchange(x, "space")
+        found = exchange(in_time, "time")
+        return add_round(exchange(spatial(x), "space"), found)
+
+    tokens, in_time = lax.cond(core == 0, lead, follow, packed)
     tokens, passed = lax.optimization_barrier((tokens, swap_cores(tokens[0, 0, 0, :16])))
-    tokens = lax.cond(core == 1, to_space, lambda x: x, tokens)
-    in_time = temporal(exchange(tokens, "mirrored"))
-    total = add_round(spatial(tokens), exchange(in_time, "mirrored"))
-    total = exchange(total, "space")
+    total = lax.cond(core == 0, lead_rest, follow_rest, tokens, in_time)
     return tuple(finish(scalars, total, swap_cores(total[:, 2:]), passed))
 
 

time: 252 us -> 242 us (0.960)
  starting transfers between devices: 62.1 us -> 45.3 us
  waiting for transfers between devices: 6.43 us -> 15.1 us
    ppermute x3, starting transfers between devices: 58.1 us -> 32.3 us  [swap_cores(): return lax.ppermute(value, AXES, [(int(a), int(b)) for a, b in pairs])]
    all_to_all x1, waiting for transfers between devices: 3.75 us -> 12.8 us  [exchange(): lax.all_to_all(value, AXES, split_axis=0, concat_axis=0, tiled=True, axis...]
    all_to_all x1, starting transfers between devices: 4.03 us -> 13 us  [exchange(): lax.all_to_all(value, AXES, split_axis=0, concat_axis=0, tiled=True, axis...]
where the time goes in v5:
time: 242 us; the launch traced here: 241 us
  blocking collectives  138 us (57%)
  starting transfers between devices  45.3 us (19%)
  Pallas kernels  39 us (16%)
  waiting for transfers between devices  15.1 us (6%)
    all_to_all x3, blocking collectives, exchange(): lax.all_to_all(value, AXES, split_axis=0, concat_axis=0, tiled=True, axis...  138 us
    ppermute x3, starting transfers between devices, swap_cores(): return lax.ppermute(value, AXES, [(int(a), int(b)) for a, b in pairs])  32.3 us
    pallas_call x1, Pallas kernels, spatial(): pl.pallas_call(spatial_kernel, grid=(4,), in_specs=[pl.BlockSpec((16, 3,...  15.7 us
    pallas_call x4, Pallas kernels, call(): pl.pallas_call(kernel, grid_spec=pltpu.PrefetchScalarGridSpec(num_scalar_...  15.2 us
    all_to_all x1, starting transfers between devices, exchange(): lax.all_to_all(value, AXES, split_axis=0, concat_axis=0, tiled=True, axis...  13 us
    all_to_all x1, waiting for transfers between devices, exchange(): lax.all_to_all(value, AXES, split_axis=0, concat_axis=0, tiled=True, axis...  12.8 us
    pallas_call x1, Pallas kernels, temporal(): pl.pallas_call(temporal_kernel, grid=(4,), in_specs=[pl.BlockSpec((16, 3,...  8.1 us
  transfers between devices with their start and end apart: 4, of which 3 were waited for; matrix products, arithmetic and copies ran while one was open for 0% of the time, Pallas kernels for 8%

profile of v5, /device:TPU:1, one launch (start us, length us, event | category | flops | bytes accessed | tf_op | source)
XLA Modules:
  0.0 241.0 jit_solution(4263764841544203898)
XLA Ops:
  0.7 0.7 pad_add_fusion.s
  1.3 3.2 %other_heads.1 = bf16[6,2,64,1024]{3,2,1,0:T(8,128)(2,1)} custom-call(s32[3]{0:T(128)} %pad_add_fusion.s, bf16[2,64,2048]{2,1,0:T(8,128)(2,1)} %refs_0_.3, bf16[2,64,2048]{2,1,0:T(8,128)(2,1)} %refs_1_.3, bf16[2,64,2048]{2,1,0:T(8,128)(2,1)} %refs_2_.3, bf16[2,64,2048]{2,1,0:T(8,128)(2,1)} %refs_3_.3, bf16[2,64,2048]{2,1,0:T(8,128)(2,1)} %refs_4_.3, ...), custom_call_target="tpu_custom_call" | custom-call | bytes 1024 | tf_op jit(solution)/shard_map/other_heads/pallas_call | solution.py:55
  4.5 8.8 %collective-permute-start = (bf16[6,2,64,1024]{3,2,1,0:T(8,128)(2,1)}, bf16[6,2,64,1024]{3,2,1,0:T(8,128)(2,1)}, u32[]{:S(2)}, u32[]{:S(2)}) collective-permute-start(bf16[6,2,64,1024]{3,2,1,0:T(8,128)(2,1)} %other_heads.1), channel_id=1, source_target_pairs={{0,16},{1,17},{2,18},{3,19},{4,20},{5,21},{6,22},{7,23},{8,24},{9,... | collective-permute-start | bytes 4718600 | tf_op jit(solution)/shard_map/ppermute | solution.py:51
  13.3 3.8 %pack_own.1.refs_6_ = bf16[16,3,4,64,128]{4,3,2,1,0:T(8,128)(2,1)S(1)} custom-call(s32[3]{0:T(128)} %pad_add_fusion.s, bf16[2,64,2048]{2,1,0:T(8,128)(2,1)} %refs_0_.3, bf16[2,64,2048]{2,1,0:T(8,128)(2,1)} %refs_1_.3, bf16[2,64,2048]{2,1,0:T(8,128)(2,1)} %refs_2_.3, bf16[2,64,2048]{2,1,0:T(8,128)(2,1)} %refs_3_.3, bf16[2,64,2048]{2,1,0:T(8,128)(2,1)} %refs_4_.3, ...), custom_call_target="tpu_custom_call" | custom-call | bytes 1024 | tf_op jit(solution)/shard_map/pack_own/pallas_call | solution.py:55
  17.1 0.0 collective-permute-done.refs_0_.refs_1_.refs_2_.refs_3_.refs_4_.refs_5_
  17.1 3.7 %pack_other.1 = bf16[16,3,4,64,128]{4,3,2,1,0:T(8,128)(2,1)S(1)} custom-call(s32[3]{0:T(128)} %pad_add_fusion.s, bf16[6,2,64,1024]{3,2,1,0:T(8,128)(2,1)} %collective-permute-done.refs_0_.refs_1_.refs_2_.refs_3_.refs_4_.refs_5_, ...), custom_call_target="tpu_custom_call", output_to_operand_aliasing={{}: (7, {})} | custom-call | bytes 1024 | tf_op jit(solution)/shard_map/pack_other/pallas_call | solution.py:55
  20.8 62.1 %conditional.2 = (bf16[16,3,4,64,128]{4,3,2,1,0:T(8,128)(2,1)S(1)}, bf16[16,4,64,128]{3,2,1,0:T(8,128)(2,1)S(1)}) conditional(s32[]{:T(128)} %convert_element_type.22, bf16[16,3,4,64,128]{4,3,2,1,0:T(8,128)(2,1)S(1)} %pack_other.1, bf16[16,3,4,64,128]{4,3,2,1,0:T(8,128)(2,1)S(1)} %pack_other.1), branch_computations={%region_0.1_spmd, %region_1.2_spmd} | conditional | bytes 13631506 | solution.py:269
  20.8 54.0 %all_to_all.32.x_ref = bf16[16,3,4,64,128]{4,3,2,1,0:T(8,128)(2,1)S(1)} all-to-all(bf16[16,3,4,64,128]{4,3,2,1,0:T(8,128)(2,1)S(1)} %param), channel_id=1, replica_groups={{0,32,64,96,128,160,192,224,256,288,320,352,384,416,448,480},{1,33,65,9..., dimensions={0} | all-to-all | bytes 6291456 | tf_op jit(solution)/shard_map/cond/branch_0_fun/all_to_all | solution.py:43
  74.9 8.1 %temporal.2 = bf16[16,4,64,128]{3,2,1,0:T(8,128)(2,1)S(1)} custom-call(bf16[16,3,4,64,128]{4,3,2,1,0:T(8,128)(2,1)S(1)} %all_to_all.32.x_ref), custom_call_target="tpu_custom_call" | custom-call | bytes 1024 | tf_op jit(solution)/shard_map/cond/branch_0_fun/temporal/pallas_call | solution.py:202
  83.0 19.8 %collective-permute-start.1 = (bf16[16,128]{1,0:T(8,128)(2,1)S(1)}, bf16[16,128]{1,0:T(8,128)(2,1)S(1)}, u32[]{:S(2)}, u32[]{:S(2)}) collective-permute-start(bf16[16,128]{1,0:T(8,128)(2,1)S(1)} %slice_bitcast_fusion), channel_id=1, source_target_pairs={{0,16},{1,17},{2,18},{3,19},{4,20},{5,21},{6,22},{7,23},{8,24},{9,... | collective-permute-start | bytes 12296 | tf_op jit(solution)/shard_map/ppermute | solution.py:51
  102.8 0.8 collective-permute-done.1.after_ref
  103.6 0.0 copy-start.3
  103.6 0.6 copy-done.3
  104.2 126.2 %conditional.3 = (bf16[16,4,64,128]{3,2,1,0:T(8,128)(2,1)S(1)}) conditional(s32[]{:T(128)} %convert_element_type.22, (bf16[16,3,4,64,128]{4,3,2,1,0:T(8,128)(2,1)S(1)}, bf16[16,4,64,128]{3,2,1,0:T(8,128)(2,1)S(1)}) %conditional.2, bf16[16,3,4,64,128]{4,3,2,1,0:T(8,128)(2,1)S(1)} %get-tuple-element.19), branch_computations={%region_2.3_spmd, %region_3.4_spmd} | conditional | flops 2097152 | bytes 27265092 | solution.py:271
  104.2 0.0 copy-start.1
  104.2 49.2 %all_to_all.34.x_ref = bf16[16,3,4,64,128]{4,3,2,1,0:T(8,128)(2,1)} all-to-all(bf16[16,3,4,64,128]{4,3,2,1,0:T(8,128)(2,1)S(1)} %get-tuple-element.10), channel_id=1, replica_groups={{0,1,2,3,4,5,6,7,8,9,10,11,12,13,14,15},{32,33,34,35,36,37,38,39,40,41,..., dimensions={0} | all-to-all | bytes 6291456 | tf_op jit(solution)/shard_map/cond/branch_0_fun/all_to_all | solution.py:43
  153.4 0.0 copy-done.1
  153.4 13.0 %all-to-all-start.4 = ((bf16[16,4,64,128]{3,2,1,0:T(8,128)(2,1)}), bf16[16,4,64,128]{3,2,1,0:T(8,128)(2,1)S(1)}, u32[]{:S(2)}, u32[]{:S(2)}) async-start(bf16[16,4,64,128]{3,2,1,0:T(8,128)(2,1)} %copy-done.1), calls=%async_computation.4 | async-start | bytes 2097152 | tf_op jit(solution)/shard_map/cond/branch_0_fun/all_to_all | solution.py:43
  166.4 15.7 %spatial.2 = bf16[16,4,64,128]{3,2,1,0:T(8,128)(2,1)S(1)} custom-call(bf16[16,3,4,64,128]{4,3,2,1,0:T(8,128)(2,1)} %all_to_all.34.x_ref), custom_call_target="tpu_custom_call" | custom-call | bytes 1024 | tf_op jit(solution)/shard_map/cond/branch_0_fun/spatial/pallas_call | solution.py:155
  182.1 12.8 %all-to-all-done.4 = bf16[16,4,64,128]{3,2,1,0:T(8,128)(2,1)S(1)} async-done(((bf16[16,4,64,128]{3,2,1,0:T(8,128)(2,1)}), bf16[16,4,64,128]{3,2,1,0:T(8,128)(2,1)S(1)}, u32[]{:S(2)}, u32[]{:S(2)}) %all-to-all-start.4) | async-done | bytes 1048608 | tf_op jit(solution)/shard_map/cond/branch_0_fun/all_to_all | solution.py:43
  194.9 34.9 %all_to_all.35 = bf16[16,4,64,128]{3,2,1,0:T(8,128)(2,1)S(1)} all-to-all(bf16[16,4,64,128]{3,2,1,0:T(8,128)(2,1)S(1)} %spatial.2), channel_id=1, replica_groups={{0,1,2,3,4,5,6,7,8,9,10,11,12,13,14,15},{32,33,34,35,36,37,38,39,40,41,..., dimensions={0} | all-to-all | bytes 2097152 | tf_op jit(solution)/shard_map/cond/branch_0_fun/all_to_all | solution.py:43
  229.8 0.4 add_convert_fusion
  230.5 3.7 %collective-permute-start.2 = (bf16[16,2,64,128]{3,2,1,0:T(8,128)(2,1)S(1)}, bf16[16,2,64,128]{3,2,1,0:T(8,128)(2,1)S(1)}, u32[]{:S(2)}, u32[]{:S(2)}) collective-permute-start(bf16[16,2,64,128]{3,2,1,0:T(8,128)(2,1)S(1)} %slice.8), channel_id=1, source_target_pairs={{0,16},{1,17},{2,18},{3,19},{4,20},{5,21},{6,22},{7,23},{8,24},{9,... | collective-permute-start | bytes 1572872 | tf_op jit(solution)/shard_map/ppermute | solution.py:51
  234.2 1.5 collective-permute-done.2.other_ref
  235.7 0.0 copy-start.2
  235.7 0.8 copy-done.2
  236.5 4.5 %finish.1 = (bf16[2,64,2048]{2,1,0:T(8,128)(2,1)}, bf16[2,64,2048]{2,1,0:T(8,128)(2,1)}) custom-call(s32[3]{0:T(128)} %pad_add_fusion.s, bf16[16,4,64,128]{3,2,1,0:T(8,128)(2,1)S(1)} %get-tuple-element.26.value_ref, bf16[16,2,64,128]{3,2,1,0:T(8,128)(2,1)} %copy-done.2, bf16[16,128]{1,0:T(8,128)(2,1)} %copy-done.3), custom_call_target="tpu_custom_call" | custom-call | bytes 1024 | tf_op jit(solution)/shard_map/finish/pallas_call | solution.py:55
  (2 shorter events, 0.0 us)
Async XLA Ops:
  4.5 12.6 %collective-permute-start = (bf16[6,2,64,1024]{3,2,1,0:T(8,128)(2,1)}, bf16[6,2,64,1024]{3,2,1,0:T(8,128)(2,1)}, u32[]{:S(2)}, u32[]{:S(2)}) collective-permute-start(bf16[6,2,64,1024]{3,2,1,0:T(8,128)(2,1)} %other_heads.1), channel_id=1, source_target_pairs={{0,16},{1,17},{2,18},{3,19},{4,20},{5,21},{6,22},{7,23},{8,24},{9,... | collective-permute-start | bytes 4718600 | tf_op jit(solution)/shard_map/ppermute | solution.py:51
  83.0 20.6 %collective-permute-start.1 = (bf16[16,128]{1,0:T(8,128)(2,1)S(1)}, bf16[16,128]{1,0:T(8,128)(2,1)S(1)}, u32[]{:S(2)}, u32[]{:S(2)}) collective-permute-start(bf16[16,128]{1,0:T(8,128)(2,1)S(1)} %slice_bitcast_fusion), channel_id=1, source_target_pairs={{0,16},{1,17},{2,18},{3,19},{4,20},{5,21},{6,22},{7,23},{8,24},{9,... | collective-permute-start | bytes 12296 | tf_op jit(solution)/shard_map/ppermute | solution.py:51
  103.6 0.6 copy-start.3
  104.2 49.2 %copy-start.1 = (bf16[16,4,64,128]{3,2,1,0:T(8,128)(2,1)}, bf16[16,4,64,128]{3,2,1,0:T(8,128)(2,1)S(1)}, u32[]{:S(2)}) copy-start(bf16[16,4,64,128]{3,2,1,0:T(8,128)(2,1)S(1)} %get-tuple-element.11) | copy-start | bytes 3145732 | tf_op jit(solution)/shard_map/cond
  153.4 41.5 %all-to-all-start.4 = ((bf16[16,4,64,128]{3,2,1,0:T(8,128)(2,1)}), bf16[16,4,64,128]{3,2,1,0:T(8,128)(2,1)S(1)}, u32[]{:S(2)}, u32[]{:S(2)}) async-start(bf16[16,4,64,128]{3,2,1,0:T(8,128)(2,1)} %copy-done.1), calls=%async_computation.4 | async-start | bytes 2097152 | tf_op jit(solution)/shard_map/cond/branch_0_fun/all_to_all | solution.py:43
  230.5 5.3 %collective-permute-start.2 = (bf16[16,2,64,128]{3,2,1,0:T(8,128)(2,1)S(1)}, bf16[16,2,64,128]{3,2,1,0:T(8,128)(2,1)S(1)}, u32[]{:S(2)}, u32[]{:S(2)}) collective-permute-start(bf16[16,2,64,128]{3,2,1,0:T(8,128)(2,1)S(1)} %slice.8), channel_id=1, source_target_pairs={{0,16},{1,17},{2,18},{3,19},{4,20},{5,21},{6,22},{7,23},{8,24},{9,... | collective-permute-start | bytes 1572872 | tf_op jit(solution)/shard_map/ppermute | solution.py:51
  235.7 0.8 copy-start.2

commit v6 on v5

--- a/solution.py
+++ b/solution.py
@@ -255,20 +255,18 @@
         return exchange(x, "space"), jnp.zeros((16, 4) + ROW, BF16)
 
     def follow(x):
-        return x, temporal(exchange(x, "time"))
+        return x, exchange(temporal(exchange(x, "time")), "time")
 
     def lead_rest(x, _):
         found = exchange(temporal(exchange(x, "mirrored")), "mirrored")
         return exchange(add_round(spatial(x), found), "space")
 
-    def follow_rest(x, in_time):
-        x = exchange(x, "space")
-        found = exchange(in_time, "time")
-        return add_round(exchange(spatial(x), "space"), found)
-
-    tokens, in_time = lax.cond(core == 0, lead, follow, packed)
+    def follow_rest(x, found):
+        return add_round(exchange(spatial(exchange(x, "space")), "space"), found)
+
+    tokens, found = lax.cond(core == 0, lead, follow, packed)
     tokens, passed = lax.optimization_barrier((tokens, swap_cores(tokens[0, 0, 0, :16])))
-    total = lax.cond(core == 0, lead_rest, follow_rest, tokens, in_time)
+    total = lax.cond(core == 0, lead_rest, follow_rest, tokens, found)
     return tuple(finish(scalars, total, swap_cores(total[:, 2:]), passed))
 
 

time: 242 us -> 237 us (0.979)
  blocking collectives: 138 us -> 156 us
  waiting for transfers between devices: 15.1 us -> 2.65 us
  starting transfers between devices: 45.3 us -> 34.3 us
    all_to_all x3 -> x4, blocking collectives: 138 us -> 156 us  [exchange(): lax.all_to_all(value, AXES, split_axis=0, concat_axis=0, tiled=True, axis...]
    all_to_all x1 -> x0, starting transfers between devices: 13 us -> none  [exchange(): lax.all_to_all(value, AXES, split_axis=0, concat_axis=0, tiled=True, axis...]
    all_to_all x1 -> x0, waiting for transfers between devices: 12.8 us -> none  [exchange(): lax.all_to_all(value, AXES, split_axis=0, concat_axis=0, tiled=True, axis...]
  transfers between devices with their start and end apart: 4 -> 3, of which waited for: 3 -> 2; matrix products, arithmetic and copies ran while one was open for 0% -> 0% of each run, Pallas kernels for 8% -> 2%
where the time goes in v6:
time: 237 us
  blocking collectives  156 us (66%)
  Pallas kernels  39.7 us (17%)
  starting transfers between devices  34.3 us (14%)
  waiting for transfers between devices  2.65 us (1%)
    all_to_all x4, blocking collectives, exchange(): lax.all_to_all(value, AXES, split_axis=0, concat_axis=0, tiled=True, axis...  156 us
    ppermute x3, starting transfers between devices, swap_cores(): return lax.ppermute(value, AXES, [(int(a), int(b)) for a, b in pairs])  34.3 us
    pallas_call x1, Pallas kernels, spatial(): pl.pallas_call(spatial_kernel, grid=(4,), in_specs=[pl.BlockSpec((16, 3,...  15.7 us
    pallas_call x4, Pallas kernels, call(): pl.pallas_call(kernel, grid_spec=pltpu.PrefetchScalarGridSpec(num_scalar_...  15.1 us
    pallas_call x1, Pallas kernels, temporal(): pl.pallas_call(temporal_kernel, grid=(4,), in_specs=[pl.BlockSpec((16, 3,...  8.84 us
  transfers between devices with their start and end apart: 3, of which 2 were waited for; matrix products, arithmetic and copies ran while one was open for 0% of the time, Pallas kernels for 2%

profile of v6, /device:TPU:1, one launch (start us, length us, event | category | flops | bytes accessed | tf_op | source)
XLA Modules:
  0.0 236.5 jit_solution(14455727097869085132)
XLA Ops:
  0.7 0.6 pad_add_fusion.s
  1.3 3.2 %other_heads.1 = bf16[6,2,64,1024]{3,2,1,0:T(8,128)(2,1)} custom-call(s32[3]{0:T(128)} %pad_add_fusion.s, bf16[2,64,2048]{2,1,0:T(8,128)(2,1)} %refs_0_.3, bf16[2,64,2048]{2,1,0:T(8,128)(2,1)} %refs_1_.3, bf16[2,64,2048]{2,1,0:T(8,128)(2,1)} %refs_2_.3, bf16[2,64,2048]{2,1,0:T(8,128)(2,1)} %refs_3_.3, bf16[2,64,2048]{2,1,0:T(8,128)(2,1)} %refs_4_.3, ...), custom_call_target="tpu_custom_call" | custom-call | bytes 1024 | tf_op jit(solution)/shard_map/other_heads/pallas_call | solution.py:55
  4.5 8.8 %collective-permute-start = (bf16[6,2,64,1024]{3,2,1,0:T(8,128)(2,1)}, bf16[6,2,64,1024]{3,2,1,0:T(8,128)(2,1)}, u32[]{:S(2)}, u32[]{:S(2)}) collective-permute-start(bf16[6,2,64,1024]{3,2,1,0:T(8,128)(2,1)} %other_heads.1), channel_id=1, source_target_pairs={{0,16},{1,17},{2,18},{3,19},{4,20},{5,21},{6,22},{7,23},{8,24},{9,... | collective-permute-start | bytes 4718600 | tf_op jit(solution)/shard_map/ppermute | solution.py:51
  13.2 3.8 %pack_own.1.refs_6_ = bf16[16,3,4,64,128]{4,3,2,1,0:T(8,128)(2,1)S(1)} custom-call(s32[3]{0:T(128)} %pad_add_fusion.s, bf16[2,64,2048]{2,1,0:T(8,128)(2,1)} %refs_0_.3, bf16[2,64,2048]{2,1,0:T(8,128)(2,1)} %refs_1_.3, bf16[2,64,2048]{2,1,0:T(8,128)(2,1)} %refs_2_.3, bf16[2,64,2048]{2,1,0:T(8,128)(2,1)} %refs_3_.3, bf16[2,64,2048]{2,1,0:T(8,128)(2,1)} %refs_4_.3, ...), custom_call_target="tpu_custom_call" | custom-call | bytes 1024 | tf_op jit(solution)/shard_map/pack_own/pallas_call | solution.py:55
  17.0 0.0 collective-permute-done.refs_0_.refs_1_.refs_2_.refs_3_.refs_4_.refs_5_
  17.1 3.7 %pack_other.1 = bf16[16,3,4,64,128]{4,3,2,1,0:T(8,128)(2,1)S(1)} custom-call(s32[3]{0:T(128)} %pad_add_fusion.s, bf16[6,2,64,1024]{3,2,1,0:T(8,128)(2,1)} %collective-permute-done.refs_0_.refs_1_.refs_2_.refs_3_.refs_4_.refs_5_, ...), custom_call_target="tpu_custom_call", output_to_operand_aliasing={{}: (7, {})} | custom-call | bytes 1024 | tf_op jit(solution)/shard_map/pack_other/pallas_call | solution.py:55
  20.8 88.7 %conditional.2 = (bf16[16,3,4,64,128]{4,3,2,1,0:T(8,128)(2,1)S(1)}, bf16[16,4,64,128]{3,2,1,0:T(8,128)(2,1)S(1)}) conditional(s32[]{:T(128)} %convert_element_type.22, bf16[16,3,4,64,128]{4,3,2,1,0:T(8,128)(2,1)S(1)} %pack_other.1, bf16[16,3,4,64,128]{4,3,2,1,0:T(8,128)(2,1)S(1)} %pack_other.1), branch_computations={%region_0.1_spmd, %region_1.2_spmd} | conditional | bytes 13631506 | solution.py:267
  20.8 54.2 %all_to_all.32.x_ref = bf16[16,3,4,64,128]{4,3,2,1,0:T(8,128)(2,1)} all-to-all(bf16[16,3,4,64,128]{4,3,2,1,0:T(8,128)(2,1)S(1)} %param), channel_id=1, replica_groups={{0,32,64,96,128,160,192,224,256,288,320,352,384,416,448,480},{1,33,65,9..., dimensions={0} | all-to-all | bytes 6291456 | tf_op jit(solution)/shard_map/cond/branch_0_fun/all_to_all | solution.py:43
  74.9 8.8 %temporal.2 = bf16[16,4,64,128]{3,2,1,0:T(8,128)(2,1)S(1)} custom-call(bf16[16,3,4,64,128]{4,3,2,1,0:T(8,128)(2,1)} %all_to_all.32.x_ref), custom_call_target="tpu_custom_call" | custom-call | bytes 1024 | tf_op jit(solution)/shard_map/cond/branch_0_fun/temporal/pallas_call | solution.py:202
  83.8 25.7 %all_to_all.33 = bf16[16,4,64,128]{3,2,1,0:T(8,128)(2,1)S(1)} all-to-all(bf16[16,4,64,128]{3,2,1,0:T(8,128)(2,1)S(1)} %temporal.2), channel_id=1, replica_groups={{0,32,64,96,128,160,192,224,256,288,320,352,384,416,448,480},{1,33,65,9..., dimensions={0} | all-to-all | bytes 2097152 | tf_op jit(solution)/shard_map/cond/branch_0_fun/all_to_all | solution.py:43
  109.4 1.9 collective-permute-start.1
  111.4 1.1 collective-permute-done.1.after_ref
  112.5 0.0 copy-start.2
  112.5 0.6 copy-done.2
  113.1 92.9 %conditional.3 = (bf16[16,4,64,128]{3,2,1,0:T(8,128)(2,1)S(1)}) conditional(s32[]{:T(128)} %convert_element_type.22, (bf16[16,3,4,64,128]{4,3,2,1,0:T(8,128)(2,1)S(1)}, bf16[16,4,64,128]{3,2,1,0:T(8,128)(2,1)S(1)}) %conditional.2, bf16[16,3,4,64,128]{4,3,2,1,0:T(8,128)(2,1)S(1)} %get-tuple-element.19), branch_computations={%region_2.3_spmd, %region_3.4_spmd} | conditional | flops 2097152 | bytes 27265092 | solution.py:269
  113.1 54.7 %all_to_all.35.x_ref = bf16[16,3,4,64,128]{4,3,2,1,0:T(8,128)(2,1)} all-to-all(bf16[16,3,4,64,128]{4,3,2,1,0:T(8,128)(2,1)S(1)} %get-tuple-element.10), channel_id=1, replica_groups={{0,1,2,3,4,5,6,7,8,9,10,11,12,13,14,15},{32,33,34,35,36,37,38,39,40,41,..., dimensions={0} | all-to-all | bytes 6291456 | tf_op jit(solution)/shard_map/cond/branch_0_fun/all_to_all | solution.py:43
  167.8 15.7 %spatial.2 = bf16[16,4,64,128]{3,2,1,0:T(8,128)(2,1)S(1)} custom-call(bf16[16,3,4,64,128]{4,3,2,1,0:T(8,128)(2,1)} %all_to_all.35.x_ref), custom_call_target="tpu_custom_call" | custom-call | bytes 1024 | tf_op jit(solution)/shard_map/cond/branch_0_fun/spatial/pallas_call | solution.py:155
  183.5 21.8 %all_to_all.36 = bf16[16,4,64,128]{3,2,1,0:T(8,128)(2,1)S(1)} all-to-all(bf16[16,4,64,128]{3,2,1,0:T(8,128)(2,1)S(1)} %spatial.2), channel_id=1, replica_groups={{0,1,2,3,4,5,6,7,8,9,10,11,12,13,14,15},{32,33,34,35,36,37,38,39,40,41,..., dimensions={0} | all-to-all | bytes 2097152 | tf_op jit(solution)/shard_map/cond/branch_0_fun/all_to_all | solution.py:43
  205.3 0.5 add_convert_fusion
  206.1 23.6 %collective-permute-start.2 = (bf16[16,2,64,128]{3,2,1,0:T(8,128)(2,1)S(1)}, bf16[16,2,64,128]{3,2,1,0:T(8,128)(2,1)S(1)}, u32[]{:S(2)}, u32[]{:S(2)}) collective-permute-start(bf16[16,2,64,128]{3,2,1,0:T(8,128)(2,1)S(1)} %slice.8), channel_id=1, source_target_pairs={{0,16},{1,17},{2,18},{3,19},{4,20},{5,21},{6,22},{7,23},{8,24},{9,... | collective-permute-start | bytes 1572872 | tf_op jit(solution)/shard_map/ppermute | solution.py:51
  229.7 1.5 collective-permute-done.2.other_ref
  231.2 0.0 copy-start.1
  231.2 0.8 copy-done.1
  232.0 4.5 %finish.1 = (bf16[2,64,2048]{2,1,0:T(8,128)(2,1)}, bf16[2,64,2048]{2,1,0:T(8,128)(2,1)}) custom-call(s32[3]{0:T(128)} %pad_add_fusion.s, bf16[16,4,64,128]{3,2,1,0:T(8,128)(2,1)S(1)} %get-tuple-element.26.value_ref, bf16[16,2,64,128]{3,2,1,0:T(8,128)(2,1)} %copy-done.1, bf16[16,128]{1,0:T(8,128)(2,1)} %copy-done.2), custom_call_target="tpu_custom_call" | custom-call | bytes 1024 | tf_op jit(solution)/shard_map/finish/pallas_call | solution.py:55
  (2 shorter events, 0.0 us)
Async XLA Ops:
  4.5 12.6 %collective-permute-start = (bf16[6,2,64,1024]{3,2,1,0:T(8,128)(2,1)}, bf16[6,2,64,1024]{3,2,1,0:T(8,128)(2,1)}, u32[]{:S(2)}, u32[]{:S(2)}) collective-permute-start(bf16[6,2,64,1024]{3,2,1,0:T(8,128)(2,1)} %other_heads.1), channel_id=1, source_target_pairs={{0,16},{1,17},{2,18},{3,19},{4,20},{5,21},{6,22},{7,23},{8,24},{9,... | collective-permute-start | bytes 4718600 | tf_op jit(solution)/shard_map/ppermute | solution.py:51
  109.4 3.0 %collective-permute-start.1 = (bf16[16,128]{1,0:T(8,128)(2,1)S(1)}, bf16[16,128]{1,0:T(8,128)(2,1)S(1)}, u32[]{:S(2)}, u32[]{:S(2)}) collective-permute-start(bf16[16,128]{1,0:T(8,128)(2,1)S(1)} %slice_bitcast_fusion), channel_id=1, source_target_pairs={{0,16},{1,17},{2,18},{3,19},{4,20},{5,21},{6,22},{7,23},{8,24},{9,... | collective-permute-start | bytes 12296 | tf_op jit(solution)/shard_map/ppermute | solution.py:51
  112.5 0.6 copy-start.2
  206.1 25.2 %collective-permute-start.2 = (bf16[16,2,64,128]{3,2,1,0:T(8,128)(2,1)S(1)}, bf16[16,2,64,128]{3,2,1,0:T(8,128)(2,1)S(1)}, u32[]{:S(2)}, u32[]{:S(2)}) collective-permute-start(bf16[16,2,64,128]{3,2,1,0:T(8,128)(2,1)S(1)} %slice.8), channel_id=1, source_target_pairs={{0,16},{1,17},{2,18},{3,19},{4,20},{5,21},{6,22},{7,23},{8,24},{9,... | collective-permute-start | bytes 1572872 | tf_op jit(solution)/shard_map/ppermute | solution.py:51
  231.2 0.8 copy-start.1

commit v7 on v6

--- a/solution.py
+++ b/solution.py
@@ -215,8 +215,8 @@
     return (a.astype(F32) + b.astype(F32)).astype(BF16)
 
 
-def finish(scalars, value, other, after):
-    def kernel(s, value_ref, other_ref, after_ref, out_ref, d_out_ref):
+def finish(scalars, value, other):
+    def kernel(s, value_ref, other_ref, out_ref, d_out_ref):
         swap = swap_lanes()
         side = pl.program_id(0) // 2
         flip = jnp.where(side == 0, s[1], s[2])
@@ -236,10 +236,9 @@
     block = (8, 2) + ROW
     result = pl.BlockSpec((2, 64, 512), lambda n, s: (0, 0, 2 * ((n // 2) ^ s[0]) + n % 2))
     return call(
-        kernel, scalars, [value, other, after], (4,),
+        kernel, scalars, [value, other], (4,),
         [pl.BlockSpec(block, lambda n, s: (jnp.minimum(n, 1), 0, 0, 0)),
-         pl.BlockSpec(block, lambda n, s: (jnp.maximum(n - 2, 0), 0, 0, 0)),
-         pl.BlockSpec(memory_space=pl.ANY)],
+         pl.BlockSpec(block, lambda n, s: (jnp.maximum(n - 2, 0), 0, 0, 0))],
         [result, result], [out_like(2, 64, 2048)] * 2, "finish")
 
 
@@ -265,9 +264,8 @@
         return add_round(exchange(spatial(exchange(x, "space")), "space"), found)
 
     tokens, found = lax.cond(core == 0, lead, follow, packed)
-    tokens, passed = lax.optimization_barrier((tokens, swap_cores(tokens[0, 0, 0, :16])))
     total = lax.cond(core == 0, lead_rest, follow_rest, tokens, found)
-    return tuple(finish(scalars, total, swap_cores(total[:, 2:]), passed))
+    return tuple(finish(scalars, total, swap_cores(total[:, 2:])))
 
 
 def solution(mesh):

time: 237 us -> 234 us (0.987)
    ppermute x3 -> x2, starting transfers between devices: 34.3 us -> 32.7 us  [swap_cores(): return lax.ppermute(value, AXES, [(int(a), int(b)) for a, b in pairs])]
  transfers between devices with their start and end apart: 3 -> 2, of which waited for: 2 -> 1; matrix products, arithmetic and copies ran while one was open for 0% -> 0% of each run, Pallas kernels for 2% -> 2%
where the time goes in v7:
time: 234 us; the launch traced here: 233 us
  blocking collectives  156 us (67%)
  Pallas kernels  39.6 us (17%)
  starting transfers between devices  32.7 us (14%)
    all_to_all x4, blocking collectives, exchange(): lax.all_to_all(value, AXES, split_axis=0, concat_axis=0, tiled=True, axis...  156 us
    ppermute x2, starting transfers between devices, swap_cores(): return lax.ppermute(value, AXES, [(int(a), int(b)) for a, b in pairs])  32.7 us
    pallas_call x1, Pallas kernels, spatial(): pl.pallas_call(spatial_kernel, grid=(4,), in_specs=[pl.BlockSpec((16, 3,...  15.7 us
    pallas_call x4, Pallas kernels, call(): pl.pallas_call(kernel, grid_spec=pltpu.PrefetchScalarGridSpec(num_scalar_...  15.1 us
    pallas_call x1, Pallas kernels, temporal(): pl.pallas_call(temporal_kernel, grid=(4,), in_specs=[pl.BlockSpec((16, 3,...  8.84 us
  transfers between devices with their start and end apart: 2, of which 1 were waited for; matrix products, arithmetic and copies ran while one was open for 0% of the time, Pallas kernels for 2%

profile of v7, /device:TPU:1, one launch (start us, length us, event | category | flops | bytes accessed | tf_op | source)
XLA Modules:
  0.0 232.8 jit_solution(5540061415118549839)
XLA Ops:
  0.7 0.7 pad_add_fusion.s
  1.3 3.2 %other_heads.1 = bf16[6,2,64,1024]{3,2,1,0:T(8,128)(2,1)} custom-call(s32[3]{0:T(128)} %pad_add_fusion.s, bf16[2,64,2048]{2,1,0:T(8,128)(2,1)} %refs_0_.3, bf16[2,64,2048]{2,1,0:T(8,128)(2,1)} %refs_1_.3, bf16[2,64,2048]{2,1,0:T(8,128)(2,1)} %refs_2_.3, bf16[2,64,2048]{2,1,0:T(8,128)(2,1)} %refs_3_.3, bf16[2,64,2048]{2,1,0:T(8,128)(2,1)} %refs_4_.3, ...), custom_call_target="tpu_custom_call" | custom-call | bytes 1024 | tf_op jit(solution)/shard_map/other_heads/pallas_call | solution.py:55
  4.5 8.8 %collective-permute-start = (bf16[6,2,64,1024]{3,2,1,0:T(8,128)(2,1)}, bf16[6,2,64,1024]{3,2,1,0:T(8,128)(2,1)}, u32[]{:S(2)}, u32[]{:S(2)}) collective-permute-start(bf16[6,2,64,1024]{3,2,1,0:T(8,128)(2,1)} %other_heads.1), channel_id=1, source_target_pairs={{0,16},{1,17},{2,18},{3,19},{4,20},{5,21},{6,22},{7,23},{8,24},{9,... | collective-permute-start | bytes 4718600 | tf_op jit(solution)/shard_map/ppermute | solution.py:51
  13.3 3.8 %pack_own.1.refs_6_ = bf16[16,3,4,64,128]{4,3,2,1,0:T(8,128)(2,1)S(1)} custom-call(s32[3]{0:T(128)} %pad_add_fusion.s, bf16[2,64,2048]{2,1,0:T(8,128)(2,1)} %refs_0_.3, bf16[2,64,2048]{2,1,0:T(8,128)(2,1)} %refs_1_.3, bf16[2,64,2048]{2,1,0:T(8,128)(2,1)} %refs_2_.3, bf16[2,64,2048]{2,1,0:T(8,128)(2,1)} %refs_3_.3, bf16[2,64,2048]{2,1,0:T(8,128)(2,1)} %refs_4_.3, ...), custom_call_target="tpu_custom_call" | custom-call | bytes 1024 | tf_op jit(solution)/shard_map/pack_own/pallas_call | solution.py:55
  17.1 0.0 collective-permute-done.refs_0_.refs_1_.refs_2_.refs_3_.refs_4_.refs_5_
  17.1 3.7 %pack_other.1 = bf16[16,3,4,64,128]{4,3,2,1,0:T(8,128)(2,1)S(1)} custom-call(s32[3]{0:T(128)} %pad_add_fusion.s, bf16[6,2,64,1024]{3,2,1,0:T(8,128)(2,1)} %collective-permute-done.refs_0_.refs_1_.refs_2_.refs_3_.refs_4_.refs_5_, ...), custom_call_target="tpu_custom_call", output_to_operand_aliasing={{}: (7, {})} | custom-call | bytes 1024 | tf_op jit(solution)/shard_map/pack_other/pallas_call | solution.py:55
  20.8 88.7 %conditional.2 = (bf16[16,3,4,64,128]{4,3,2,1,0:T(8,128)(2,1)S(1)}, bf16[16,4,64,128]{3,2,1,0:T(8,128)(2,1)S(1)}) conditional(s32[]{:T(128)} %convert_element_type.22, bf16[16,3,4,64,128]{4,3,2,1,0:T(8,128)(2,1)S(1)} %pack_other.1, bf16[16,3,4,64,128]{4,3,2,1,0:T(8,128)(2,1)S(1)} %pack_other.1), branch_computations={%region_0.1_spmd, %region_1.2_spmd} | conditional | bytes 13631506 | solution.py:266
  20.8 54.2 %all_to_all.32.x_ref = bf16[16,3,4,64,128]{4,3,2,1,0:T(8,128)(2,1)} all-to-all(bf16[16,3,4,64,128]{4,3,2,1,0:T(8,128)(2,1)S(1)} %param), channel_id=1, replica_groups={{0,32,64,96,128,160,192,224,256,288,320,352,384,416,448,480},{1,33,65,9..., dimensions={0} | all-to-all | bytes 6291456 | tf_op jit(solution)/shard_map/cond/branch_0_fun/all_to_all | solution.py:43
  74.9 8.8 %temporal.2 = bf16[16,4,64,128]{3,2,1,0:T(8,128)(2,1)S(1)} custom-call(bf16[16,3,4,64,128]{4,3,2,1,0:T(8,128)(2,1)} %all_to_all.32.x_ref), custom_call_target="tpu_custom_call" | custom-call | bytes 1024 | tf_op jit(solution)/shard_map/cond/branch_0_fun/temporal/pallas_call | solution.py:202
  83.8 25.7 %all_to_all.33 = bf16[16,4,64,128]{3,2,1,0:T(8,128)(2,1)S(1)} all-to-all(bf16[16,4,64,128]{3,2,1,0:T(8,128)(2,1)S(1)} %temporal.2), channel_id=1, replica_groups={{0,32,64,96,128,160,192,224,256,288,320,352,384,416,448,480},{1,33,65,9..., dimensions={0} | all-to-all | bytes 2097152 | tf_op jit(solution)/shard_map/cond/branch_0_fun/all_to_all | solution.py:43
  109.4 92.6 %conditional.3 = (bf16[16,4,64,128]{3,2,1,0:T(8,128)(2,1)S(1)}) conditional(s32[]{:T(128)} %convert_element_type.22, (bf16[16,3,4,64,128]{4,3,2,1,0:T(8,128)(2,1)S(1)}, bf16[16,4,64,128]{3,2,1,0:T(8,128)(2,1)S(1)}) %conditional.2, bf16[16,3,4,64,128]{4,3,2,1,0:T(8,128)(2,1)S(1)} %get-tuple-element.15), branch_computations={%region_2.3_spmd, %region_3.4_spmd} | conditional | flops 2097152 | bytes 27265092 | solution.py:267
  109.4 54.4 %all_to_all.35.x_ref = bf16[16,3,4,64,128]{4,3,2,1,0:T(8,128)(2,1)} all-to-all(bf16[16,3,4,64,128]{4,3,2,1,0:T(8,128)(2,1)S(1)} %get-tuple-element.10), channel_id=1, replica_groups={{0,1,2,3,4,5,6,7,8,9,10,11,12,13,14,15},{32,33,34,35,36,37,38,39,40,41,..., dimensions={0} | all-to-all | bytes 6291456 | tf_op jit(solution)/shard_map/cond/branch_0_fun/all_to_all | solution.py:43
  163.9 15.7 %spatial.2 = bf16[16,4,64,128]{3,2,1,0:T(8,128)(2,1)S(1)} custom-call(bf16[16,3,4,64,128]{4,3,2,1,0:T(8,128)(2,1)} %all_to_all.35.x_ref), custom_call_target="tpu_custom_call" | custom-call | bytes 1024 | tf_op jit(solution)/shard_map/cond/branch_0_fun/spatial/pallas_call | solution.py:155
  179.6 21.7 %all_to_all.36 = bf16[16,4,64,128]{3,2,1,0:T(8,128)(2,1)S(1)} all-to-all(bf16[16,4,64,128]{3,2,1,0:T(8,128)(2,1)S(1)} %spatial.2), channel_id=1, replica_groups={{0,1,2,3,4,5,6,7,8,9,10,11,12,13,14,15},{32,33,34,35,36,37,38,39,40,41,..., dimensions={0} | all-to-all | bytes 2097152 | tf_op jit(solution)/shard_map/cond/branch_0_fun/all_to_all | solution.py:43
  201.3 0.5 add_convert_fusion
  202.1 23.9 %collective-permute-start.1 = (bf16[16,2,64,128]{3,2,1,0:T(8,128)(2,1)S(1)}, bf16[16,2,64,128]{3,2,1,0:T(8,128)(2,1)S(1)}, u32[]{:S(2)}, u32[]{:S(2)}) collective-permute-start(bf16[16,2,64,128]{3,2,1,0:T(8,128)(2,1)S(1)} %slice.4), channel_id=1, source_target_pairs={{0,16},{1,17},{2,18},{3,19},{4,20},{5,21},{6,22},{7,23},{8,24},{9,... | collective-permute-start | bytes 1572872 | tf_op jit(solution)/shard_map/ppermute | solution.py:51
  226.0 1.5 collective-permute-done.1.other_ref
  227.5 0.0 copy-start.1
  227.5 0.8 copy-done.1
  228.3 4.5 %finish.1 = (bf16[2,64,2048]{2,1,0:T(8,128)(2,1)}, bf16[2,64,2048]{2,1,0:T(8,128)(2,1)}) custom-call(s32[3]{0:T(128)} %pad_add_fusion.s, bf16[16,4,64,128]{3,2,1,0:T(8,128)(2,1)S(1)} %get-tuple-element.20.value_ref, bf16[16,2,64,128]{3,2,1,0:T(8,128)(2,1)} %copy-done.1), custom_call_target="tpu_custom_call" | custom-call | bytes 1024 | tf_op jit(solution)/shard_map/finish/pallas_call | solution.py:55
  (1 shorter events, 0.0 us)
Async XLA Ops:
  4.5 12.6 %collective-permute-start = (bf16[6,2,64,1024]{3,2,1,0:T(8,128)(2,1)}, bf16[6,2,64,1024]{3,2,1,0:T(8,128)(2,1)}, u32[]{:S(2)}, u32[]{:S(2)}) collective-permute-start(bf16[6,2,64,1024]{3,2,1,0:T(8,128)(2,1)} %other_heads.1), channel_id=1, source_target_pairs={{0,16},{1,17},{2,18},{3,19},{4,20},{5,21},{6,22},{7,23},{8,24},{9,... | collective-permute-start | bytes 4718600 | tf_op jit(solution)/shard_map/ppermute | solution.py:51
  202.1 25.4 %collective-permute-start.1 = (bf16[16,2,64,128]{3,2,1,0:T(8,128)(2,1)S(1)}, bf16[16,2,64,128]{3,2,1,0:T(8,128)(2,1)S(1)}, u32[]{:S(2)}, u32[]{:S(2)}) collective-permute-start(bf16[16,2,64,128]{3,2,1,0:T(8,128)(2,1)S(1)} %slice.4), channel_id=1, source_target_pairs={{0,16},{1,17},{2,18},{3,19},{4,20},{5,21},{6,22},{7,23},{8,24},{9,... | collective-permute-start | bytes 1572872 | tf_op jit(solution)/shard_map/ppermute | solution.py:51
  227.5 0.8 copy-start.1
